TPU v7x, 32 devices: a whole 2x2x4 slice. The times are simulated.
32 devices in a mesh: parts: 2 (over y), shard: 4 (over z), grp: 2 (over x), sub: 2 (over core).
Axes of the slice: x: 2, y: 2, z: 4, core: 2. Of those that a mesh axis runs over, the one named last changes fastest.
Arguments:
- embeddings: float32 [16384, 1024], P(('parts', 'shard', 'grp', 'sub')), parts along dimension 0, may hold values from -120 to 120
- labels: int32 [16384], P(('parts', 'shard', 'grp', 'sub')), parts along dimension 0, may hold values from 0 to 4095, as said below
- doc_block: int32 [16384], P(('parts', 'shard', 'grp', 'sub')), parts along dimension 0, may hold values from 0 to 3
- assign: int32 [8192], P('parts'), parts along dimension 0, may hold values from 0 to 3, as said below
- pattern: int32 [4, 4], replicated, may hold values 0 or 1
Outputs:
- doc_max: float32 [16384], P(('parts', 'shard', 'grp', 'sub')), parts along dimension 0
There are 2 independent parts, one for each index of `parts`. A program takes and returns all parts, laid end to end along the dimension named above; an argument that names none is the same for every part. Nothing has to cross between parts.
Inputs may be any that keep to these rules, and one draw needn't show every extreme that they name: `labels`: in each aligned block of 512 documents (the documents of one device) at most 256 have a cluster that assign maps to any one group; one group, the same for every block of a part, gets exactly 256 from every block. Split the clusters of a group, starting at cluster s with e clusters, into 4 ranges, range k holding clusters s + (k * e) // 4 up to the start of range k + 1; of the documents that one block sends to one group at most 64 fall into any one range, and the group that gets 256 from every block gets exactly that many in every range. `assign`: Non-decreasing over the clusters; every group owns at least 8 clusters.
All inputs are finite; a program needn't handle non-finite values.
Results may differ from a plain program's by a relative error of at most 0.0003.
Values may be sent and summed in bfloat16 or wider, within the bound.
No kernel may reach another device: no remote copies, remote signals or barrier semaphores. Data moves between devices by JAX's collectives and lax.ppermute only.
A program may use at most 64 MiB of HBM per device.

v0:
```python
import jax
import jax.numpy as jnp
from jax import lax
from jax.sharding import PartitionSpec as P


def row_masks(doc_codes, pattern):
    count = pattern.shape[0]
    powers = jnp.left_shift(jnp.int32(1), jnp.arange(count, dtype=jnp.int32))
    pattern_bits = jnp.sum(pattern * powers[None, :], axis=1)
    block_ids = doc_codes % count
    picked = block_ids[:, None] == jnp.arange(count, dtype=jnp.int32)[None, :]
    return jnp.sum(jnp.where(picked, pattern_bits[None, :], 0), axis=1)


def allowed(row_codes, masks, col_codes, count):
    adjacent = jnp.abs(row_codes[:, None] // count - col_codes[None, :] // count) <= 1
    filled = (col_codes >= 0)[None, :]
    permitted = jnp.right_shift(masks[:, None], col_codes[None, :] % count) % 2 == 1
    return adjacent & filled & permitted


def scores(left_rows, right_rows):
    return lax.dot_general(
        left_rows, right_rows, (((1,), (1,)), ((), ())), preferred_element_type=jnp.float32
    )


def per_device(embeddings, labels, doc_block, assign, pattern):
    count = pattern.shape[0]
    group_count = lax.axis_size("shard")
    local_rows = embeddings.shape[0]
    capacity = 2 * local_rows // group_count
    features = embeddings.shape[1]
    unit_rows = (
        embeddings * lax.rsqrt(jnp.sum(embeddings * embeddings, axis=1, keepdims=True) + 1e-06)
    ).astype(jnp.bfloat16)
    target_group = assign[labels]
    one_hot = (target_group[:, None] == jnp.arange(group_count, dtype=jnp.int32)[None, :]).astype(
        jnp.int32
    )
    earlier = jnp.cumsum(one_hot, axis=0) - one_hot
    send_slot = target_group * capacity + jnp.sum(earlier * one_hot, axis=1)
    doc_codes = labels * count + doc_block
    outgoing = (
        jnp.zeros((group_count * capacity, features), jnp.bfloat16).at[send_slot].set(unit_rows)
    )
    outgoing_codes = jnp.full((group_count * capacity,), -1, jnp.int32).at[send_slot].set(doc_codes)
    arrived, arrived_codes = (
        lax.all_to_all(outgoing, "shard", split_axis=0, concat_axis=0, tiled=True),
        lax.all_to_all(outgoing_codes, "shard", split_axis=0, concat_axis=0, tiled=True),
    )
    masks = row_masks(arrived_codes, pattern)
    row_count = arrived.shape[0]
    position = lax.axis_index(("grp", "sub")) * row_count + jnp.arange(row_count, dtype=jnp.int32)
    start_value = jnp.full((row_count,), -1.0, jnp.float32)
    columns = lax.all_gather(arrived, ("grp", "sub"), axis=0, tiled=True)
    column_codes = lax.all_gather(arrived_codes, ("grp", "sub"), axis=0, tiled=True)
    similarity = scores(arrived, columns)
    permitted_pairs = allowed(arrived_codes, masks, column_codes, count)
    column_position = jnp.arange(columns.shape[0], dtype=jnp.int32)
    permitted_pairs = permitted_pairs & (position[:, None] != column_position[None, :])
    best_match = jnp.maximum(
        start_value, jnp.max(jnp.where(permitted_pairs, similarity, -1.0), axis=1)
    )
    returned_max = lax.all_to_all(best_match, "shard", split_axis=0, concat_axis=0, tiled=True)
    return returned_max[send_slot]


def solution(mesh):
    in_specs = (
        P(("parts", "shard", "grp", "sub"), None),
        P(("parts", "shard", "grp", "sub")),
        P(("parts", "shard", "grp", "sub")),
        P("parts"),
        P(),
    )
    out_specs = P(("parts", "shard", "grp", "sub"))
    return jax.shard_map(
        per_device, mesh=mesh, in_specs=in_specs, out_specs=out_specs, check_vma=False
    )
```

profile of v0, /device:TPU:0, one launch (start us, length us, event | category | flops | bytes accessed | tf_op | source)
XLA Modules:
  0.0 177.2 jit_solution(1994156326158213957)
XLA Ops:
  6.5 0.0 copy-start
  6.5 0.0 copy-start.1
  6.5 0.0 all-gather.2.cloned.1.call-start
  6.5 0.9 multiply_add_fusion
  7.4 0.0 copy-done
  7.4 3.1 %gather_fusion = s32[512]{0:T(512)S(1)} fusion(s32[4096]{0:T(1024)S(1)} %copy-done, s32[1024]{0:T(1024)S(1)} %pad_clamp_fusion.1), kind=kCustom, calls=%fused_computation | custom fusion | bytes 6144 | tf_op jit(solution)/shard_map/gather | solution.py:38
  10.6 1.2 reduce-window.6
  11.8 0.2 slice_reduce_fusion
  12.0 0.2 reduce-window.9
  12.2 0.1 add_bitcast_fusion
  12.3 1.8 %multiply_reduce_fusion = f32[512]{0:T(512)S(1)} fusion(f32[512,1024]{1,0:T(8,128)} %param.5), kind=kLoop, calls=%fused_computation.18 | loop fusion | flops 1048064 | bytes 2099200 | tf_op jit(solution)/shard_map/reduce_sum | solution.py:36
  14.1 0.0 copy-done.1
  14.1 4.2 %scatter_custom_fusion.1 = bf16[1024,1024]{1,0:T(8,128)(2,1)} fusion(s32[512]{0:T(512)S(1)} %bitcast.37, f32[512,1024]{1,0:T(8,128)S(1)} %copy-done.1, f32[512]{0:T(512)S(1)} %add_rsqrt_fusion, bf16[]{:T(256)} %constant.87.clone.1), kind=kCustom, calls=%fused_computation.19 | custom fusion | flops 1048576 | bytes 4196354 | tf_op jit(solution)/shard_map/scatter | solution.py:46
  18.4 0.0 copy-start.2
  18.4 54.7 %all_to_all.33 = bf16[4,256,1024]{2,1,0:T(8,128)(2,1)} all-to-all(bf16[4,256,1024]{2,1,0:T(8,128)(2,1)} %bitcast.33), channel_id=1, replica_groups=mesh['parts'=2,'shard'=4,'grp'=2,'sub'=2] {'shard'}, dimensions={0} | all-to-all | bytes 4194304 | tf_op jit(solution)/shard_map/all_to_all | solution.py:50
  73.1 0.0 all-gather.2.cloned.1.call-update
  73.1 3.0 %scatter_custom_fusion = s32[1024]{0:T(1024)} fusion(s32[512]{0:T(512)S(1)} %bitcast.38, s32[512]{0:T(512)S(1)} %get-tuple-element.9, s32[]{:T(128)} %constant.77.clone.1), kind=kCustom, calls=%fused_computation.60 | custom fusion | bytes 4100 | tf_op jit(solution)/shard_map/scatter | solution.py:48
  76.2 3.2 %all-to-all-start = ((s32[4,256,1]{1,2,0:T(1,128)}), s32[4,256,1]{1,2,0:T(1,128)S(1)}, u32[]{:S(2)}, u32[]{:S(2)}) async-start(s32[4,256,1]{1,2,0:T(1,128)} %bitcast.4), calls=%async_computation | async-start | bytes 8192 | tf_op jit(solution)/shard_map/all_to_all | solution.py:51
  79.4 0.0 copy-done.2
  79.4 0.1 multiply_reduce_fusion.1
  79.5 5.4 %all-to-all-done = s32[4,256,1]{1,2,0:T(1,128)S(1)} async-done(((s32[4,256,1]{1,2,0:T(1,128)}), s32[4,256,1]{1,2,0:T(1,128)S(1)}, u32[]{:S(2)}, u32[]{:S(2)}) %all-to-all-start) | async-done | bytes 4128 | tf_op jit(solution)/shard_map/all_to_all | solution.py:51
  84.9 5.4 %all_gather.6 = s32[4096]{0:T(1024)S(1)} all-gather(s32[1024]{0:T(1024)S(1)} %bitcast.34), channel_id=1, replica_groups=mesh['parts'=2,'shard'=4,'grp'=2,'sub'=2] {'grp','sub'}, dimensions={0}, use_global_device_ids=true | all-gather | bytes 20480 | tf_op jit(solution)/shard_map/all_gather | solution.py:58
  90.3 0.1 select_reduce_fusion.1
  90.5 40.4 %all-gather.2.cloned.1.call-done = bf16[4096,1024]{1,0:T(8,128)(2,1)} async-done(((bf16[1024,1024]{1,0:T(8,128)(2,1)}), bf16[4096,1024]{1,0:T(8,128)(2,1)}) %all-gather.2.cloned.1.call-update) | async-done | bytes 8388624 | tf_op jit(solution)/shard_map/all_gather | solution.py:57
  130.9 25.3 %select_reduce_fusion = f32[1024]{0:T(1024)S(1)} fusion(s32[1024]{0:T(1024)S(1)} %get-tuple-element.11, s32[4096]{0:T(1024)S(1)} %get-tuple-element.6, s32[1024]{0:T(1024)S(1)} %select_reduce_fusion.1, s32[4096]{0:T(1024)S(1)} %get-tuple-element.5, s32[1024]{0:T(1024)S(1)} %get-tuple-element.7, pred[4096]{0:T(1024)(128)(4,1)S(1)} %broadcast_compare_fusion, ...), kind=kOutput, calls=%fused_computation.11 | convolution fusion | flops 8682208256 | bytes 10539008 | tf_op jit(solution)/shard_map/dot_general | solution.py:24
  156.2 0.6 broadcast_maximum_fusion
  156.8 4.6 %all-to-all-start.2 = ((f32[4,256,1]{1,2,0:T(1,128)}), f32[4,256,1]{1,2,0:T(1,128)S(1)}, u32[]{:S(2)}, u32[]{:S(2)}) async-start(f32[4,256,1]{1,2,0:T(1,128)} %bitcast.8), calls=%async_computation.2 | async-start | bytes 8192 | tf_op jit(solution)/shard_map/all_to_all | solution.py:66
  161.4 5.6 %all-to-all-done.2 = f32[4,256,1]{1,2,0:T(1,128)S(1)} async-done(((f32[4,256,1]{1,2,0:T(1,128)}), f32[4,256,1]{1,2,0:T(1,128)S(1)}, u32[]{:S(2)}, u32[]{:S(2)}) %all-to-all-start.2) | async-done | bytes 4128 | tf_op jit(solution)/shard_map/all_to_all | solution.py:66
  167.0 3.4 %gather_fusion.1 = f32[512]{0:T(512)} fusion(f32[1024]{0:T(1024)S(1)} %bitcast.30, s32[1024]{0:T(1024)S(1)} %pad_clamp_fusion), kind=kCustom, calls=%fused_computation.1 | custom fusion | bytes 6144 | tf_op jit(solution)/shard_map/gather | solution.py:67
  (11 shorter events, 0.1 us)
Async XLA Ops:
  6.5 0.9 copy-start
  6.5 7.6 %copy-start.1 = (f32[512,1024]{1,0:T(8,128)S(1)}, f32[512,1024]{1,0:T(8,128)}, u32[]{:S(2)}) copy-start(f32[512,1024]{1,0:T(8,128)} %param.5) | copy-start | bytes 6291460
  6.5 124.4 %all-gather.2.cloned.1.call-start = ((), (), s32[]{:S(2)}) async-start(), calls=%async_computation.3 | async-start | bytes 10485760 | tf_op jit(solution)/shard_map/all_gather | solution.py:57
  18.4 61.0 %copy-start.2 = (s32[4,4]{1,0:T(4,128)S(1)}, s32[4,4]{1,0:T(4,128)}, u32[]{:S(2)}) copy-start(s32[4,4]{1,0:T(4,128)} %param.9) | copy-start | bytes 196
  76.2 8.8 %all-to-all-start = ((s32[4,256,1]{1,2,0:T(1,128)}), s32[4,256,1]{1,2,0:T(1,128)S(1)}, u32[]{:S(2)}, u32[]{:S(2)}) async-start(s32[4,256,1]{1,2,0:T(1,128)} %bitcast.4), calls=%async_computation | async-start | bytes 8192 | tf_op jit(solution)/shard_map/all_to_all | solution.py:51
  156.8 10.2 %all-to-all-start.2 = ((f32[4,256,1]{1,2,0:T(1,128)}), f32[4,256,1]{1,2,0:T(1,128)S(1)}, u32[]{:S(2)}, u32[]{:S(2)}) async-start(f32[4,256,1]{1,2,0:T(1,128)} %bitcast.8), calls=%async_computation.2 | async-start | bytes 8192 | tf_op jit(solution)/shard_map/all_to_all | solution.py:66
Sparse Core Ops, SparseCore 0:
  73.3 57.5 all-gather.1
where the time goes:
time: 178 us; the launch traced here: 177 us
  blocking collectives  60.1 us (34%)
  waiting for transfers between devices  51.4 us (29%)
  matrix products  25.3 us (14%)
  between operations  13.5 us (8%)
  local copies, waits for them, and re-layouts  9.79 us (5%)
  other arithmetic  9.25 us (5%)
  starting transfers between devices  7.81 us (4%)
    all_to_all x1, blocking collectives, per_device(): lax.all_to_all(outgoing, 'shard', split_axis=0, concat_axis=0, tiled=True)  54.7 us
    all_gather x1, waiting for transfers between devices, per_device(): columns = lax.all_gather(arrived, ('grp', 'sub'), axis=0, tiled=True)  40.4 us
    dot_general x1, matrix products, scores(): lax.dot_general(left_rows, right_rows, (((1,), (1,)), ((), ())), preferre...  25.3 us
    all_to_all x1, waiting for transfers between devices, per_device(): lax.all_to_all(best_match, 'shard', split_axis=0, concat_axis=0, tiled=True)  5.57 us
    all_to_all x1, waiting for transfers between devices, per_device(): lax.all_to_all(outgoing_codes, 'shard', split_axis=0, concat_axis=0, tile...  5.4 us
    all_gather x1, blocking collectives, per_device(): lax.all_gather(arrived_codes, ('grp', 'sub'), axis=0, tiled=True)  5.39 us
    all_to_all x1, starting transfers between devices, per_device(): lax.all_to_all(best_match, 'shard', split_axis=0, concat_axis=0, tiled=True)  4.59 us
    scatter x1, other arithmetic, per_device(): jnp.zeros((group_count * capacity, features), jnp.bfloat16).at[send_slot]  4.22 us
  transfers between devices with their start and end apart: 3, of which 3 were waited for; matrix products, arithmetic and copies ran while one was open for 2% of the time, Pallas kernels for 0%

commit v1 on v0

--- a/solution.py
+++ b/solution.py
@@ -1,7 +1,18 @@
+import functools
+import math
+
 import jax
 import jax.numpy as jnp
 from jax import lax
+from jax.experimental import pallas as pl
+from jax.experimental.pallas import tpu as pltpu
 from jax.sharding import PartitionSpec as P
+
+BF16 = jnp.bfloat16
+F32 = jnp.float32
+VMEM_LIMIT = 48 * 1024 * 1024
+LANES = 128
+BARRED = 4.0
 
 
 def row_masks(doc_codes, pattern):
@@ -26,7 +37,13 @@
     )
 
 
-def per_device(embeddings, labels, doc_block, assign, pattern):
+def from_members(rows):
+    members = lax.axis_size(("grp", "sub"))
+    shifts = [[(i, (i + shift) % members) for i in range(members)] for shift in range(1, members)]
+    return jnp.concatenate([rows] + [lax.ppermute(rows, ("grp", "sub"), to) for to in shifts])
+
+
+def general_form(embeddings, labels, doc_block, assign, pattern):
     count = pattern.shape[0]
     group_count = lax.axis_size("shard")
     local_rows = embeddings.shape[0]
@@ -52,10 +69,10 @@
     )
     masks = row_masks(arrived_codes, pattern)
     row_count = arrived.shape[0]
-    position = lax.axis_index(("grp", "sub")) * row_count + jnp.arange(row_count, dtype=jnp.int32)
+    position = jnp.arange(row_count, dtype=jnp.int32)
     start_value = jnp.full((row_count,), -1.0, jnp.float32)
-    columns = lax.all_gather(arrived, ("grp", "sub"), axis=0, tiled=True)
-    column_codes = lax.all_gather(arrived_codes, ("grp", "sub"), axis=0, tiled=True)
+    columns = from_members(arrived)
+    column_codes = from_members(arrived_codes)
     similarity = scores(arrived, columns)
     permitted_pairs = allowed(arrived_codes, masks, column_codes, count)
     column_position = jnp.arange(columns.shape[0], dtype=jnp.int32)
@@ -65,6 +82,243 @@
     )
     returned_max = lax.all_to_all(best_match, "shard", split_axis=0, concat_axis=0, tiled=True)
     return returned_max[send_slot]
+
+
+def dot_nt(left, right):
+    return lax.dot_general(left, right, (((1,), (1,)), ((), ())), preferred_element_type=F32)
+
+
+def pack_kernel(
+    groups, chips, cores, slots, count, emb_ref, label_ref, block_ref, assign_ref, out_ref, slot_ref
+):
+    docs, features = emb_ref.shape
+    part = features // cores
+    labels = label_ref[...]
+    clusters = assign_ref.shape[0] * assign_ref.shape[1]
+    assign = assign_ref[...]
+
+    group = jnp.zeros((1, docs), jnp.int32)
+    start = jnp.zeros((1, docs), jnp.int32)
+    stop = jnp.full((1, docs), clusters, jnp.int32)
+    for g in range(1, groups):
+        bound = jnp.sum((assign < g).astype(F32), axis=0, keepdims=True)
+        bound = jnp.sum(bound, axis=1, keepdims=True).astype(jnp.int32)
+        inside = labels >= bound
+        group = group + inside.astype(jnp.int32)
+        start = jnp.where(inside, jnp.maximum(start, bound), start)
+        stop = jnp.where(inside, stop, jnp.minimum(stop, bound))
+    extent = (stop - start).astype(F32)
+
+    def home_of(cluster):
+        above = ((cluster - start + 1) * chips - 1).astype(F32)
+        return jnp.floor((above + 0.5) / extent).astype(jnp.int32)
+
+    home = home_of(labels)
+    beside = jnp.where(labels + 1 < stop, home_of(labels + 1), home)
+
+    chip_id = lax.broadcasted_iota(jnp.int32, (chips, docs), 0)
+    member = (chip_id == home) | (chip_id == beside)
+    earlier = (
+        lax.broadcasted_iota(jnp.int32, (docs, docs), 0)
+        < lax.broadcasted_iota(jnp.int32, (docs, docs), 1)
+    ).astype(F32).astype(BF16)
+    rank = jnp.dot(
+        member.astype(F32).astype(BF16), earlier, preferred_element_type=F32
+    ).astype(jnp.int32)
+    over = jnp.max((member & (rank >= slots - 1)).astype(F32), axis=0, keepdims=True)
+    over = jnp.max(over, axis=1, keepdims=True)
+    slot = jnp.where(member & (rank < slots - 1), rank, -1)
+    slot_ref[...] = slot
+
+    code = (labels + group) * count + block_ref[...] + 1
+    row_id = lax.broadcasted_iota(jnp.int32, (8, docs), 0)
+    digits = jnp.where(row_id == 0, code >> 7, jnp.where(row_id == 1, code & 127, 0))
+    digits = digits.astype(F32).astype(BF16)
+
+    slot_id = lax.broadcasted_iota(jnp.int32, (chips, slots, docs), 1)
+    picks = (slot_id == slot[:, None, :]).astype(F32).reshape(chips * slots, docs).astype(BF16)
+
+    lane_slot = lax.broadcasted_iota(jnp.int32, (LANES, docs), 0)
+    code_rows = []
+    for chip in range(chips):
+        pick = (lane_slot == slot[chip : chip + 1, :]).astype(F32).astype(BF16)
+        sent = dot_nt(digits, pick)
+        row = [sent[0:1, :], sent[1:2, :], jnp.broadcast_to(over, (1, LANES))]
+        row.append(jnp.zeros((1, part - 3 * LANES), F32))
+        code_rows.append(jnp.concatenate(row, axis=1))
+    code_rows = jnp.concatenate(code_rows, axis=0)
+
+    emb = emb_ref[...]
+    unit = (emb * lax.rsqrt(jnp.sum(emb * emb, axis=1, keepdims=True) + 1e-06)).astype(BF16)
+    last = lax.broadcasted_iota(jnp.int32, (chips, slots, part), 1) == slots - 1
+    for core in range(cores):
+        rows = jnp.dot(
+            picks, unit[:, core * part : (core + 1) * part], preferred_element_type=F32
+        ).reshape(chips, slots, part)
+        rows = jnp.where(last, code_rows[:, None, :], rows).reshape(chips * slots, part)
+        out_ref[core * chips * slots : (core + 1) * chips * slots, :] = rows.astype(BF16)
+
+
+def match_kernel(
+    chips, cores, slots, core_ref, own_ref, other_ref, pattern_ref, best_ref, code_ref
+):
+    half = chips * slots
+    total = cores * half
+    core = core_ref[0]
+    sources = cores * chips
+
+    at_row = lax.broadcasted_iota(jnp.int32, (sources, total), 1)
+    source = lax.broadcasted_iota(jnp.int32, (sources, total), 0)
+    pick = (at_row == source * slots + slots - 1).astype(F32).astype(BF16)
+    sent = jnp.dot(pick, own_ref[:, : 2 * LANES], preferred_element_type=F32)
+    lane_of = lax.broadcasted_iota(jnp.int32, (LANES, total), 0)
+    col_of = lax.broadcasted_iota(jnp.int32, (LANES, total), 1)
+    spread = (lane_of == lax.rem(col_of, slots)).astype(F32).astype(BF16)
+    mine = lax.div(at_row, slots) == source
+    high = jnp.dot(sent[:, :LANES].astype(BF16), spread, preferred_element_type=F32)
+    low = jnp.dot(sent[:, LANES : 2 * LANES].astype(BF16), spread, preferred_element_type=F32)
+    code = jnp.sum(jnp.where(mine, high * 128.0 + low, 0.0), axis=0, keepdims=True) - 1.0
+    count = pattern_ref.shape[0]
+    label = jnp.floor((code + 0.5) / count)
+    label = jnp.where(code < 0.0, -8.0, label)
+    block = jnp.where(code < 0.0, -1.0, code - label * count)
+
+    code_ref[:, 0:1] = jnp.transpose(jnp.broadcast_to(label, (8, total)))[:, 0:1]
+    code_ref[:, 1:2] = jnp.transpose(jnp.broadcast_to(block, (8, total)))[:, 0:1]
+
+    lane = lax.broadcasted_iota(jnp.int32, (half, LANES), 1).astype(F32)
+    wide = jnp.zeros((LANES, LANES), F32)
+    from_block = lax.broadcasted_iota(jnp.int32, (LANES, LANES), 0)
+    to_block = lax.broadcasted_iota(jnp.int32, (LANES, LANES), 1)
+    for a in range(count):
+        for b in range(count):
+            term = BARRED * (pattern_ref[a, b].astype(F32) - 1.0)
+            wide = jnp.where((from_block == a) & (to_block == b), term, wide)
+    base = pl.multiple_of(core * half, 16)
+    row_label = code_ref[pl.ds(base, half), 0:1]
+    row_hot = (lane == code_ref[pl.ds(base, half), 1:2]).astype(F32).astype(BF16)
+    row_terms = jnp.dot(row_hot, wide.astype(BF16), preferred_element_type=F32).astype(BF16)
+    row_label = jnp.broadcast_to(row_label, (half, LANES))
+    left_own = own_ref[pl.ds(base, half), :]
+    left_other = other_ref[pl.ds(base, half), :]
+
+    best = jnp.full((half, LANES), -1.0, F32)
+    row_at = lax.broadcasted_iota(jnp.int32, (half, LANES), 0)
+    col_at = lax.broadcasted_iota(jnp.int32, (half, LANES), 1)
+    step = 2 * LANES
+    label_cols = jnp.broadcast_to(label, (8, total))
+    for turn in range(cores):
+        which = lax.rem(core + turn, cores)
+        begin = pl.multiple_of(which * half, 16)
+        labels_here = label_cols[:, 0:half]
+        for k in range(1, cores):
+            labels_here = jnp.where(which == k, label_cols[:, k * half : (k + 1) * half], labels_here)
+        for at in range(0, half, step):
+            width = min(step, half - at)
+            offset = pl.multiple_of(begin + at, 16)
+            sim = dot_nt(left_own, own_ref[pl.ds(offset, width), :])
+            sim += dot_nt(left_other, other_ref[pl.ds(offset, width), :])
+            lane_w = lax.broadcasted_iota(jnp.int32, (width, LANES), 1).astype(F32)
+            hot = (lane_w == code_ref[pl.ds(offset, width), 1:2]).astype(F32).astype(BF16)
+            sim += dot_nt(row_terms, hot)
+            for piece in range(0, width, LANES):
+                span = min(LANES, width - piece)
+                gap = row_label[:, :span] - labels_here[0:1, at + piece : at + piece + span]
+                near = jnp.abs(gap) <= 1.0
+                if turn == 0:
+                    near = near & (row_at[:, :span] != col_at[:, :span] + (at + piece))
+                value = jnp.where(near, sim[:, piece : piece + span], -1.0)
+                if span < LANES:
+                    value = jnp.concatenate(
+                        [value, jnp.full((half, LANES - span), -1.0, F32)], axis=1
+                    )
+                best = jnp.maximum(best, value)
+    across = jnp.max(jnp.transpose(best), axis=0, keepdims=True)
+    for chip in range(chips):
+        best_ref[chip : chip + 1, 0:slots] = across[:, chip * slots : (chip + 1) * slots]
+
+
+def unpack_kernel(chips, slots, back_ref, slot_ref, out_ref):
+    docs = slot_ref.shape[1]
+    back = jnp.transpose(back_ref[...])
+    slot_id = lax.broadcasted_iota(jnp.int32, (slots, docs), 0)
+    best = jnp.full((slots, docs), -1.0, F32)
+    for chip in range(chips):
+        here = slot_id == slot_ref[chip : chip + 1, :]
+        best = jnp.maximum(best, jnp.where(here, back[0:slots, chip : chip + 1], -1.0))
+    out_ref[...] = jnp.max(best, axis=0, keepdims=True)
+
+
+def in_vmem():
+    return pl.BlockSpec(memory_space=pltpu.VMEM)
+
+
+def in_smem():
+    return pl.BlockSpec(memory_space=pltpu.SMEM)
+
+
+def per_device(embeddings, labels, doc_block, assign, pattern):
+    groups = lax.axis_size("shard")
+    chips = groups * lax.axis_size("grp")
+    cores = lax.axis_size("sub")
+    docs, features = embeddings.shape
+    count = pattern.shape[0]
+    mean = docs // chips
+    slots = -(-(mean + int(3 * math.sqrt(mean))) // 8) * 8
+    half = chips * slots
+    part = features // cores
+    params = pltpu.CompilerParams(vmem_limit_bytes=VMEM_LIMIT)
+
+    outgoing, slot = pl.pallas_call(
+        functools.partial(pack_kernel, groups, chips, cores, slots, count),
+        out_shape=(
+            jax.ShapeDtypeStruct((cores * half, part), BF16),
+            jax.ShapeDtypeStruct((chips, docs), jnp.int32),
+        ),
+        in_specs=[in_vmem()] * 4,
+        out_specs=(in_vmem(), in_vmem()),
+        compiler_params=params,
+        name="pack",
+    )(
+        embeddings,
+        labels.reshape(1, docs),
+        doc_block.reshape(1, docs),
+        assign.reshape(-1, LANES),
+    )
+    arrived = lax.all_to_all(
+        outgoing, ("sub", "shard", "grp"), split_axis=0, concat_axis=0, tiled=True
+    )
+    swapped = lax.ppermute(arrived, "sub", [(i, (i + 1) % cores) for i in range(cores)])
+    core = lax.axis_index("sub").astype(jnp.int32).reshape(1)
+    over = arrived.reshape(cores * chips, slots, part)[:, slots - 1, 2 * LANES : 3 * LANES]
+    over = jnp.max(over.astype(F32), axis=0, keepdims=True)
+    parts = lax.axis_size("parts")
+    for shift in range(1, parts):
+        to = [(i, (i + shift) % parts) for i in range(parts)]
+        over = jnp.maximum(over, lax.ppermute(over, "parts", to))
+    best = pl.pallas_call(
+        functools.partial(match_kernel, chips, cores, slots),
+        out_shape=jax.ShapeDtypeStruct((chips, LANES), F32),
+        in_specs=[in_smem(), in_vmem(), in_vmem(), in_smem()],
+        out_specs=in_vmem(),
+        scratch_shapes=[pltpu.VMEM((cores * half, LANES), F32)],
+        compiler_params=params,
+        name="match",
+    )(core, arrived, swapped, pattern)
+    back = lax.all_to_all(best, ("shard", "grp"), split_axis=0, concat_axis=0, tiled=True)
+    found = pl.pallas_call(
+        functools.partial(unpack_kernel, chips, slots),
+        out_shape=jax.ShapeDtypeStruct((1, docs), F32),
+        in_specs=[in_vmem()] * 2,
+        out_specs=in_vmem(),
+        compiler_params=params,
+        name="unpack",
+    )(back, slot).reshape(docs)
+    return lax.cond(
+        over[0, 0] > 0.0,
+        lambda: general_form(embeddings, labels, doc_block, assign, pattern),
+        lambda: found,
+    )
 
 
 def solution(mesh):

time: 178 us -> 67.3 us (0.38)
  waiting for transfers between devices: 51.4 us -> 7.92 us
  matrix products: 25.3 us -> 0 us
  blocking collectives: 60.1 us -> 42.7 us
  between operations: 13.5 us -> 0.13 us
  Pallas kernels: 0 us -> 10.5 us
  other arithmetic: 9.25 us -> 0.05 us
  local copies, waits for them, and re-layouts: 9.79 us -> 0.59 us
  starting transfers between devices: 7.81 us -> 4.92 us
    all_gather x1 -> x0, waiting for transfers between devices: 40.4 us -> none  [per_device(): columns = lax.all_gather(arrived, ('grp', 'sub'), axis=0, tiled=True)]
    dot_general x1 -> x0, matrix products: 25.3 us -> none  [scores(): lax.dot_general(left_rows, right_rows, (((1,), (1,)), ((), ())), preferre...]
    all_to_all x1, blocking collectives: 54.7 us -> 42.7 us  [per_device(): lax.all_to_all(outgoing, ('sub', 'shard', 'grp'), split_axis=0, concat_ax...]
    pallas_call x0 -> x3, Pallas kernels: none -> 10.5 us  [the longest x1 7 us: per_device(): pl.pallas_call(functools.partial(match_kernel, chips, cores, slots), out_...]
    gather x2 -> x0, local copies, waits for them, and re-layouts: 6.55 us -> none  [the longest x1 3.41 us: per_device(): return returned_max[send_slot]]
    all_gather x1 -> x0, blocking collectives: 5.39 us -> none  [per_device(): lax.all_gather(arrived_codes, ('grp', 'sub'), axis=0, tiled=True)]
    all_to_all x2 -> x1, waiting for transfers between devices: 11 us -> 6.34 us  [per_device(): lax.all_to_all(best, ('shard', 'grp'), split_axis=0, concat_axis=0, tiled...]
    all_to_all x2 -> x1, starting transfers between devices: 7.81 us -> 3.33 us  [per_device(): lax.all_to_all(best, ('shard', 'grp'), split_axis=0, concat_axis=0, tiled...]
  transfers between devices with their start and end apart: 3 -> 3, of which waited for: 3 -> 2; matrix products, arithmetic and copies ran while one was open for 2% -> 0% of each run, Pallas kernels for 0% -> 10%
where the time goes in v1:
time: 67.3 us; the launch traced here: 67 us
  blocking collectives  42.7 us (63%)
  Pallas kernels  10.5 us (16%)
  waiting for transfers between devices  7.92 us (12%)
  starting transfers between devices  4.92 us (7%)
    all_to_all x1, blocking collectives, per_device(): lax.all_to_all(outgoing, ('sub', 'shard', 'grp'), split_axis=0, concat_ax...  42.7 us
    pallas_call x1, Pallas kernels, per_device(): pl.pallas_call(functools.partial(match_kernel, chips, cores, slots), out_...  7 us
    all_to_all x1, waiting for transfers between devices, per_device(): lax.all_to_all(best, ('shard', 'grp'), split_axis=0, concat_axis=0, tiled...  6.34 us
    all_to_all x1, starting transfers between devices, per_device(): lax.all_to_all(best, ('shard', 'grp'), split_axis=0, concat_axis=0, tiled...  3.33 us
    pallas_call x1, Pallas kernels, per_device(): pl.pallas_call(functools.partial(pack_kernel, groups, chips, cores, slots...  3.11 us
    ppermute x1, starting transfers between devices, per_device(): over = jnp.maximum(over, lax.ppermute(over, 'parts', to))  1.58 us
    ppermute x1, waiting for transfers between devices, per_device(): lax.ppermute(arrived, 'sub', [(i, (i + 1) % cores) for i in range(cores)])  1.58 us
  transfers between devices with their start and end apart: 3, of which 2 were waited for; matrix products, arithmetic and copies ran while one was open for 0% of the time, Pallas kernels for 10%

profile of v1, /device:TPU:0, one launch (start us, length us, event | category | flops | bytes accessed | tf_op | source)
XLA Modules:
  0.0 67.0 jit_solution(14027575133740704166)
XLA Ops:
  0.0 0.0 copy-start.2
  0.0 3.1 %pack.1 = (bf16[1408,512]{1,0:T(8,128)(2,1)S(1)}, s32[8,512]{1,0:T(8,128)S(1)}) custom-call(f32[512,1024]{1,0:T(8,128)} %emb_ref.1, s32[1,512]{1,0:T(1,128)} %bitcast.70, s32[1,512]{1,0:T(1,128)} %bitcast.71, s32[32,128]{1,0:T(8,128)} %bitcast.52), custom_call_target="tpu_custom_call" | custom-call | tf_op jit(solution)/shard_map/pack/pallas_call | solution.py:272
  3.1 42.7 %all_to_all.48 = bf16[16,88,512]{2,1,0:T(8,128)(2,1)S(1)} all-to-all(bf16[16,88,512]{2,1,0:T(8,128)(2,1)S(1)} %bitcast.49), channel_id=1, replica_groups=mesh['parts'=2,'shard'=4,'grp'=2,'sub'=2] {'sub','shard','grp'}, dimensions={0} | all-to-all | bytes 2883584 | tf_op jit(solution)/shard_map/all_to_all | solution.py:288
  45.8 0.0 copy-start
  45.8 0.0 copy-start.3
  45.8 0.0 copy-start.4
  45.8 0.0 collective-permute-start.7
  45.9 1.6 %collective-permute-start.6 = (f32[1,128]{1,0:T(1,128)S(1)}, f32[1,128]{1,0:T(1,128)S(1)}, u32[]{:S(2)}, u32[]{:S(2)}) collective-permute-start(f32[1,128]{1,0:T(1,128)S(1)} %bitcast_convert_fusion), channel_id=1, source_target_pairs={{0,16},{16,0},{1,17},{17,1},{2,18},{18,2},{3,19},{19,3},{4,20},{20... | collective-permute-start | bytes 1544 | tf_op jit(solution)/shard_map/ppermute | solution.py:298
  47.5 1.6 %collective-permute-done.7.other_ref = bf16[1408,512]{1,0:T(8,128)(2,1)S(1)} collective-permute-done((bf16[1408,512]{1,0:T(8,128)(2,1)S(1)}, bf16[1408,512]{1,0:T(8,128)(2,1)S(1)}, u32[]{:S(2)}, u32[]{:S(2)}) %collective-permute-start.7) | collective-permute-done | bytes 1441824 | tf_op jit(solution)/shard_map/ppermute | solution.py:291
  49.1 0.0 copy-done.2
  49.1 7.0 %match.1 = f32[8,128]{1,0:T(8,128)} custom-call(s32[1]{0:T(128)} %bitcast.18.core_ref, bf16[1408,512]{1,0:T(8,128)(2,1)S(1)} %bitcast.48, bf16[1408,512]{1,0:T(8,128)(2,1)S(1)} %collective-permute-done.7.other_ref, s32[4,4]{1,0:T(4,128)S(1)} %copy-done.2), custom_call_target="tpu_custom_call" | custom-call | tf_op jit(solution)/shard_map/match/pallas_call | solution.py:299
  56.1 3.3 %all-to-all-start.4 = ((f32[8,1,128]{2,1,0:T(1,128)}), f32[8,1,128]{2,1,0:T(1,128)S(1)}, u32[]{:S(2)}, u32[]{:S(2)}) async-start(f32[8,1,128]{2,1,0:T(1,128)} %bitcast.21), calls=%async_computation.4 | async-start | bytes 8192 | tf_op jit(solution)/shard_map/all_to_all | solution.py:308
  59.4 0.0 collective-permute-done.6
  59.5 6.3 %all-to-all-done.4 = f32[8,1,128]{2,1,0:T(1,128)S(1)} async-done(((f32[8,1,128]{2,1,0:T(1,128)}), f32[8,1,128]{2,1,0:T(1,128)S(1)}, u32[]{:S(2)}, u32[]{:S(2)}) %all-to-all-start.4) | async-done | bytes 4128 | tf_op jit(solution)/shard_map/all_to_all | solution.py:308
  65.8 0.4 unpack.1
  66.2 0.0 copy-done
  66.2 0.0 copy-done.3
  66.2 0.0 copy-done.4
  66.2 0.2 conditional.1
  66.5 0.0 copy-start.5
  66.5 0.6 copy-done.5
  (3 shorter events, 0.0 us)
Async XLA Ops:
  0.0 49.1 %copy-start.2 = (s32[4,4]{1,0:T(4,128)S(1)}, s32[4,4]{1,0:T(4,128)}, u32[]{:S(2)}) copy-start(s32[4,4]{1,0:T(4,128)} %pattern_ref.1) | copy-start | bytes 196
  45.8 20.4 %copy-start = (s32[4096]{0:T(1024)S(1)}, s32[4096]{0:T(1024)}, u32[]{:S(2)}) copy-start(s32[4096]{0:T(1024)} %param.10) | copy-start | bytes 49156
  45.8 20.4 %copy-start.3 = (s32[512]{0:T(512)S(1)}, s32[512]{0:T(512)}, u32[]{:S(2)}) copy-start(s32[512]{0:T(512)} %param.8) | copy-start | bytes 6148
  45.8 20.4 %copy-start.4 = (s32[512]{0:T(512)S(1)}, s32[512]{0:T(512)}, u32[]{:S(2)}) copy-start(s32[512]{0:T(512)} %param.9) | copy-start | bytes 6148
  45.8 3.2 %collective-permute-start.7 = (bf16[1408,512]{1,0:T(8,128)(2,1)S(1)}, bf16[1408,512]{1,0:T(8,128)(2,1)S(1)}, u32[]{:S(2)}, u32[]{:S(2)}) collective-permute-start(bf16[1408,512]{1,0:T(8,128)(2,1)S(1)} %bitcast.47), channel_id=1, source_target_pairs={{0,1},{1,0},{2,3},{3,2},{4,5},{5,4},{6,7},{7,6},{8,9},{9,8},{10,11... | collective-permute-start | bytes 4325384 | tf_op jit(solution)/shard_map/ppermute | solution.py:291
  45.9 13.5 %collective-permute-start.6 = (f32[1,128]{1,0:T(1,128)S(1)}, f32[1,128]{1,0:T(1,128)S(1)}, u32[]{:S(2)}, u32[]{:S(2)}) collective-permute-start(f32[1,128]{1,0:T(1,128)S(1)} %bitcast_convert_fusion), channel_id=1, source_target_pairs={{0,16},{16,0},{1,17},{17,1},{2,18},{18,2},{3,19},{19,3},{4,20},{20... | collective-permute-start | bytes 1544 | tf_op jit(solution)/shard_map/ppermute | solution.py:298
  56.1 9.7 %all-to-all-start.4 = ((f32[8,1,128]{2,1,0:T(1,128)}), f32[8,1,128]{2,1,0:T(1,128)S(1)}, u32[]{:S(2)}, u32[]{:S(2)}) async-start(f32[8,1,128]{2,1,0:T(1,128)} %bitcast.21), calls=%async_computation.4 | async-start | bytes 8192 | tf_op jit(solution)/shard_map/all_to_all | solution.py:308
  66.5 0.6 copy-start.5

commit v2 on v1

v2 whole, which is shorter than its diff:
```python
import functools
import math

import jax
import jax.numpy as jnp
from jax import lax
from jax.experimental import pallas as pl
from jax.experimental.pallas import tpu as pltpu
from jax.sharding import PartitionSpec as P

BF16 = jnp.bfloat16
F32 = jnp.float32
VMEM_LIMIT = 48 * 1024 * 1024
LANES = 128
MORE = 40
BARRED = 4.0


def row_masks(doc_codes, pattern):
    count = pattern.shape[0]
    powers = jnp.left_shift(jnp.int32(1), jnp.arange(count, dtype=jnp.int32))
    pattern_bits = jnp.sum(pattern * powers[None, :], axis=1)
    block_ids = doc_codes % count
    picked = block_ids[:, None] == jnp.arange(count, dtype=jnp.int32)[None, :]
    return jnp.sum(jnp.where(picked, pattern_bits[None, :], 0), axis=1)


def allowed(row_codes, masks, col_codes, count):
    adjacent = jnp.abs(row_codes[:, None] // count - col_codes[None, :] // count) <= 1
    filled = (col_codes >= 0)[None, :]
    permitted = jnp.right_shift(masks[:, None], col_codes[None, :] % count) % 2 == 1
    return adjacent & filled & permitted


def scores(left_rows, right_rows):
    return lax.dot_general(
        left_rows, right_rows, (((1,), (1,)), ((), ())), preferred_element_type=jnp.float32
    )


def from_members(rows):
    members = lax.axis_size(("grp", "sub"))
    shifts = [[(i, (i + shift) % members) for i in range(members)] for shift in range(1, members)]
    return jnp.concatenate([rows] + [lax.ppermute(rows, ("grp", "sub"), to) for to in shifts])


def general_form(embeddings, labels, doc_block, assign, pattern):
    count = pattern.shape[0]
    group_count = lax.axis_size("shard")
    local_rows = embeddings.shape[0]
    capacity = 2 * local_rows // group_count
    features = embeddings.shape[1]
    unit_rows = (
        embeddings * lax.rsqrt(jnp.sum(embeddings * embeddings, axis=1, keepdims=True) + 1e-06)
    ).astype(jnp.bfloat16)
    target_group = assign[labels]
    one_hot = (target_group[:, None] == jnp.arange(group_count, dtype=jnp.int32)[None, :]).astype(
        jnp.int32
    )
    earlier = jnp.cumsum(one_hot, axis=0) - one_hot
    send_slot = target_group * capacity + jnp.sum(earlier * one_hot, axis=1)
    doc_codes = labels * count + doc_block
    outgoing = (
        jnp.zeros((group_count * capacity, features), jnp.bfloat16).at[send_slot].set(unit_rows)
    )
    outgoing_codes = jnp.full((group_count * capacity,), -1, jnp.int32).at[send_slot].set(doc_codes)
    arrived, arrived_codes = (
        lax.all_to_all(outgoing, "shard", split_axis=0, concat_axis=0, tiled=True),
        lax.all_to_all(outgoing_codes, "shard", split_axis=0, concat_axis=0, tiled=True),
    )
    masks = row_masks(arrived_codes, pattern)
    row_count = arrived.shape[0]
    position = jnp.arange(row_count, dtype=jnp.int32)
    start_value = jnp.full((row_count,), -1.0, jnp.float32)
    columns = from_members(arrived)
    column_codes = from_members(arrived_codes)
    similarity = scores(arrived, columns)
    permitted_pairs = allowed(arrived_codes, masks, column_codes, count)
    column_position = jnp.arange(columns.shape[0], dtype=jnp.int32)
    permitted_pairs = permitted_pairs & (position[:, None] != column_position[None, :])
    best_match = jnp.maximum(
        start_value, jnp.max(jnp.where(permitted_pairs, similarity, -1.0), axis=1)
    )
    returned_max = lax.all_to_all(best_match, "shard", split_axis=0, concat_axis=0, tiled=True)
    return returned_max[send_slot]


def dot_nt(left, right):
    return lax.dot_general(left, right, (((1,), (1,)), ((), ())), preferred_element_type=F32)


def pack_kernel(
    groups, chips, first, slots, count, emb_ref, label_ref, block_ref, assign_ref, out_ref, slot_ref
):
    docs, features = emb_ref.shape
    labels = label_ref[...]
    clusters = assign_ref.shape[0] * assign_ref.shape[1]
    assign = assign_ref[...]

    group = jnp.zeros((1, docs), jnp.int32)
    start = jnp.zeros((1, docs), jnp.int32)
    stop = jnp.full((1, docs), clusters, jnp.int32)
    for g in range(1, groups):
        bound = jnp.sum((assign < g).astype(F32), axis=0, keepdims=True)
        bound = jnp.sum(bound, axis=1, keepdims=True).astype(jnp.int32)
        inside = labels >= bound
        group = group + inside.astype(jnp.int32)
        start = jnp.where(inside, jnp.maximum(start, bound), start)
        stop = jnp.where(inside, stop, jnp.minimum(stop, bound))
    extent = (stop - start).astype(F32)

    def home_of(cluster):
        above = ((cluster - start + 1) * chips - 1).astype(F32)
        return jnp.floor((above + 0.5) / extent).astype(jnp.int32)

    home = home_of(labels)
    beside = jnp.where(labels + 1 < stop, home_of(labels + 1), home)

    chip_id = lax.broadcasted_iota(jnp.int32, (chips, docs), 0)
    member = (chip_id == home) | (chip_id == beside)
    earlier = (
        lax.broadcasted_iota(jnp.int32, (docs, docs), 0)
        < lax.broadcasted_iota(jnp.int32, (docs, docs), 1)
    ).astype(F32).astype(BF16)
    rank = jnp.dot(
        member.astype(F32).astype(BF16), earlier, preferred_element_type=F32
    ).astype(jnp.int32) - first
    most = jnp.max(jnp.where(member, rank, -1), axis=0, keepdims=True)
    most = jnp.max(most, axis=1, keepdims=True)
    past = jnp.where(most >= slots - 1, 1.0, 0.0) + jnp.where(most >= slots + MORE - 2, 1.0, 0.0)
    slot = jnp.where(member & (rank >= 0) & (rank < slots - 1), rank, -1)
    slot_ref[...] = slot

    code = (labels + group) * count + block_ref[...] + 1
    row_id = lax.broadcasted_iota(jnp.int32, (8, docs), 0)
    digits = jnp.where(row_id == 0, code >> 7, jnp.where(row_id == 1, code & 127, 0))
    digits = digits.astype(F32).astype(BF16)

    slot_id = lax.broadcasted_iota(jnp.int32, (chips, slots, docs), 1)
    picks = (slot_id == slot[:, None, :]).astype(F32).reshape(chips * slots, docs).astype(BF16)

    lane_slot = lax.broadcasted_iota(jnp.int32, (LANES, docs), 0)
    code_rows = []
    for chip in range(chips):
        pick = (lane_slot == slot[chip : chip + 1, :]).astype(F32).astype(BF16)
        sent = dot_nt(digits, pick)
        row = [sent[0:1, :], sent[1:2, :], jnp.broadcast_to(past, (1, LANES))]
        row.append(jnp.zeros((1, features - 3 * LANES), F32))
        code_rows.append(jnp.concatenate(row, axis=1))
    code_rows = jnp.concatenate(code_rows, axis=0)

    emb = emb_ref[...]
    unit = (emb * lax.rsqrt(jnp.sum(emb * emb, axis=1, keepdims=True) + 1e-06)).astype(BF16)
    step = min(features, 4 * LANES)
    last = lax.broadcasted_iota(jnp.int32, (chips, slots, step), 1) == slots - 1
    for at in range(0, features, step):
        rows = jnp.dot(picks, unit[:, at : at + step], preferred_element_type=F32)
        rows = rows.reshape(chips, slots, step)
        rows = jnp.where(last, code_rows[:, None, at : at + step], rows)
        out_ref[:, at : at + step] = rows.reshape(chips * slots, step).astype(BF16)


def codes_of(rows_ref, chips, segments, count):
    rows = rows_ref.shape[0]
    slots = sum(segments)
    at_row = lax.broadcasted_iota(jnp.int32, (chips, rows), 1)
    chip_row = lax.broadcasted_iota(jnp.int32, (chips, rows), 0) * slots
    found, begin = [], 0
    for length in segments:
        pick = (at_row == chip_row + (begin + length - 1)).astype(F32).astype(BF16)
        sent = jnp.dot(pick, rows_ref[:, : 2 * LANES], preferred_element_type=F32)
        found.append(sent[:, :LANES] * 128.0 + sent[:, LANES:])
        begin += length
    pieces = []
    for chip in range(chips):
        for length, code in zip(segments, found):
            pieces.append(code[chip : chip + 1, :length])
    code = jnp.concatenate(pieces, axis=1) - 1.0
    label = jnp.floor((code + 0.5) / count)
    block = jnp.where(code < 0.0, -1.0, code - label * count)
    return jnp.where(code < 0.0, -8.0, label), block


def down(row):
    return jnp.transpose(jnp.broadcast_to(row, (8, row.shape[1])))[:, 0:1]


def hot_blocks(block):
    lane = lax.broadcasted_iota(jnp.int32, (block.shape[0], LANES), 1).astype(F32)
    return (lane == block).astype(F32).astype(BF16)


def match_rows(left_ref, row_label, row_terms, right_ref, label, hot, same, best):
    rows, columns = left_ref.shape[0], right_ref.shape[0]
    row_at = lax.broadcasted_iota(jnp.int32, (rows, LANES), 0)
    col_at = lax.broadcasted_iota(jnp.int32, (rows, LANES), 1)
    left = left_ref[...]
    step = 2 * LANES
    for at in range(0, columns, step):
        width = min(step, columns - at)
        sim = dot_nt(left, right_ref[at : at + width, :])
        sim += dot_nt(row_terms, hot[at : at + width, :])
        for piece in range(0, width, LANES):
            span = min(LANES, width - piece)
            near = jnp.abs(row_label[:, :span] - label[:, at + piece : at + piece + span]) <= 1.0
            if same:
                near = near & (row_at[:, :span] != col_at[:, :span] + (at + piece))
            value = jnp.where(near, sim[:, piece : piece + span], -1.0)
            if span < LANES:
                value = jnp.concatenate([value, jnp.full((rows, LANES - span), -1.0, F32)], axis=1)
            best = jnp.maximum(best, value)
    return best


def match_own_kernel(
    chips, segments, own_ref, pattern_ref, best_ref, label_ref, terms_ref
):
    rows = own_ref.shape[0]
    count = pattern_ref.shape[0]
    label, block = codes_of(own_ref, chips, segments, count)
    hot = hot_blocks(down(block))
    table = jnp.zeros((LANES, LANES), F32)
    from_block = lax.broadcasted_iota(jnp.int32, (LANES, LANES), 0)
    to_block = lax.broadcasted_iota(jnp.int32, (LANES, LANES), 1)
    for a in range(count):
        for b in range(count):
            term = BARRED * (pattern_ref[a, b].astype(F32) - 1.0)
            table = jnp.where((from_block == a) & (to_block == b), term, table)
    row_terms = jnp.dot(hot, table.astype(BF16), preferred_element_type=F32).astype(BF16)
    row_label = jnp.broadcast_to(down(label), (rows, LANES))
    label_ref[...] = row_label
    terms_ref[...] = row_terms
    best = jnp.full((rows, LANES), -1.0, F32)
    best_ref[...] = match_rows(own_ref, row_label, row_terms, own_ref, label, hot, True, best)


def match_other_kernel(
    chips, segments, count, own_ref, other_ref, before_ref, label_ref, terms_ref, best_ref
):
    slots = sum(segments)
    label, block = codes_of(other_ref, chips, segments, count)
    hot = hot_blocks(down(block))
    best = match_rows(
        own_ref, label_ref[...], terms_ref[...], other_ref, label, hot, False, before_ref[...]
    )
    across = jnp.max(jnp.transpose(best), axis=0, keepdims=True)
    for chip in range(chips):
        best_ref[chip : chip + 1, 0:slots] = across[:, chip * slots : (chip + 1) * slots]


def unpack_kernel(chips, slots, back_ref, slot_ref, out_ref):
    docs = slot_ref.shape[1]
    back = jnp.transpose(back_ref[...])
    slot_id = lax.broadcasted_iota(jnp.int32, (slots, docs), 0)
    best = jnp.full((slots, docs), -1.0, F32)
    for chip in range(chips):
        here = slot_id == slot_ref[chip : chip + 1, :]
        best = jnp.maximum(best, jnp.where(here, back[0:slots, chip : chip + 1], -1.0))
    out_ref[...] = jnp.max(best, axis=0, keepdims=True)


def in_vmem():
    return pl.BlockSpec(memory_space=pltpu.VMEM)


def in_smem():
    return pl.BlockSpec(memory_space=pltpu.SMEM)


def params():
    return pltpu.CompilerParams(vmem_limit_bytes=VMEM_LIMIT)


def cost(flops, moved):
    return pl.CostEstimate(flops=flops, bytes_accessed=moved, transcendentals=0)


def send(embeddings, labels, doc_block, assign, count, first, slots):
    groups = lax.axis_size("shard")
    chips = groups * lax.axis_size("grp")
    docs, features = embeddings.shape
    outgoing, slot = pl.pallas_call(
        functools.partial(pack_kernel, groups, chips, first, slots, count),
        out_shape=(
            jax.ShapeDtypeStruct((chips * slots, features), BF16),
            jax.ShapeDtypeStruct((chips, docs), jnp.int32),
        ),
        in_specs=[in_vmem()] * 4,
        out_specs=(in_vmem(), in_vmem()),
        compiler_params=params(),
        name="pack",
    )(
        embeddings,
        labels.reshape(1, docs),
        doc_block.reshape(1, docs),
        assign.reshape(-1, LANES),
    )
    arrived = lax.all_to_all(
        outgoing, ("shard", "grp"), split_axis=0, concat_axis=0, tiled=True
    )
    return arrived, slot


def match(arrived, slot, pattern, segments):
    chips, docs = slot.shape
    slots = sum(segments)
    rows, features = arrived.shape
    cores = lax.axis_size("sub")
    other = lax.ppermute(arrived, "sub", [(i, (i + 1) % cores) for i in range(cores)])
    work = cost(2 * rows * rows * features, 2 * rows * features)
    best, label, terms = pl.pallas_call(
        functools.partial(match_own_kernel, chips, segments),
        out_shape=(
            jax.ShapeDtypeStruct((rows, LANES), F32),
            jax.ShapeDtypeStruct((rows, LANES), F32),
            jax.ShapeDtypeStruct((rows, LANES), BF16),
        ),
        in_specs=[in_vmem(), in_smem()],
        out_specs=(in_vmem(), in_vmem(), in_vmem()),
        compiler_params=params(),
        cost_estimate=work,
        name="match_own",
    )(arrived, pattern)
    best = pl.pallas_call(
        functools.partial(match_other_kernel, chips, segments, pattern.shape[0]),
        out_shape=jax.ShapeDtypeStruct((chips, LANES), F32),
        in_specs=[in_vmem()] * 5,
        out_specs=in_vmem(),
        compiler_params=params(),
        cost_estimate=work,
        name="match_other",
    )(arrived, other, best, label, terms)
    back = lax.all_to_all(best, ("shard", "grp"), split_axis=0, concat_axis=0, tiled=True)
    return pl.pallas_call(
        functools.partial(unpack_kernel, chips, slots),
        out_shape=jax.ShapeDtypeStruct((1, docs), F32),
        in_specs=[in_vmem()] * 2,
        out_specs=in_vmem(),
        compiler_params=params(),
        name="unpack",
    )(back, slot).reshape(docs)


def per_device(embeddings, labels, doc_block, assign, pattern):
    chips = lax.axis_size("shard") * lax.axis_size("grp")
    docs, features = embeddings.shape
    count = pattern.shape[0]
    mean = docs // chips
    slots = -(-(mean + int(3 * math.sqrt(mean))) // 8) * 8
    inputs = (embeddings, labels, doc_block, assign)

    arrived, slot = send(*inputs, count, 0, slots)
    found = match(arrived, slot, pattern, (slots,))

    past = arrived.reshape(chips, slots, features)[:, slots - 1, 2 * LANES : 3 * LANES]
    past = jnp.max(past.astype(F32), axis=0, keepdims=True)
    for axis in ("sub", "parts"):
        size = lax.axis_size(axis)
        for shift in range(1, size):
            to = [(i, (i + shift) % size) for i in range(size)]
            past = jnp.maximum(past, lax.ppermute(past, axis, to))

    def second_round():
        more, more_slot = send(*inputs, count, slots - 1, MORE)
        both = jnp.concatenate(
            [arrived.reshape(chips, slots, features), more.reshape(chips, MORE, features)], axis=1
        ).reshape(chips * (slots + MORE), features)
        both_slot = jnp.where(more_slot >= 0, more_slot + slots, slot)
        return match(both, both_slot, pattern, (slots, MORE))

    return lax.cond(
        past[0, 0] > 0.0,
        lambda: lax.cond(
            past[0, 0] > 1.0, lambda: general_form(*inputs, pattern), second_round
        ),
        lambda: found,
    )


def solution(mesh):
    in_specs = (
        P(("parts", "shard", "grp", "sub"), None),
        P(("parts", "shard", "grp", "sub")),
        P(("parts", "shard", "grp", "sub")),
        P("parts"),
        P(),
    )
    out_specs = P(("parts", "shard", "grp", "sub"))
    return jax.shard_map(
        per_device, mesh=mesh, in_specs=in_specs, out_specs=out_specs, check_vma=False
    )
```

time: 67.3 us -> 62.5 us (0.929)
  waiting for transfers between devices: 7.92 us -> 4.76 us
  blocking collectives: 42.7 us -> 41.6 us
    all_to_all x1, waiting for transfers between devices: 6.34 us -> 2.74 us  [match(): lax.all_to_all(best, ('shard', 'grp'), split_axis=0, concat_axis=0, tiled...]
    all_to_all x1, blocking collectives: 42.7 us -> 41.6 us  [send(): lax.all_to_all(outgoing, ('shard', 'grp'), split_axis=0, concat_axis=0, t...]
    pallas_call x3 -> x4, Pallas kernels: 10.5 us -> 9.84 us  [the longest x1 3.08 us: send(): pl.pallas_call(functools.partial(pack_kernel, groups, chips, first, slots...]
    ppermute x2 -> x3, starting transfers between devices: 1.59 us -> 2.16 us  [the longest x2 2.16 us: per_device(): past = jnp.maximum(past, lax.ppermute(past, axis, to))]
    ppermute x2 -> x3, waiting for transfers between devices: 1.58 us -> 2.02 us  [the longest x2 2.02 us: per_device(): past = jnp.maximum(past, lax.ppermute(past, axis, to))]
  transfers between devices with their start and end apart: 3 -> 4, of which waited for: 2 -> 2; matrix products, arithmetic and copies ran while one was open for 0% -> 0% of each run, Pallas kernels for 10% -> 9%
where the time goes in v2:
time: 62.5 us; the launch traced here: 62.2 us
  blocking collectives  41.6 us (67%)
  Pallas kernels  9.84 us (16%)
  starting transfers between devices  5.41 us (9%)
  waiting for transfers between devices  4.76 us (8%)
    all_to_all x1, blocking collectives, send(): lax.all_to_all(outgoing, ('shard', 'grp'), split_axis=0, concat_axis=0, t...  41.6 us
    all_to_all x1, starting transfers between devices, match(): lax.all_to_all(best, ('shard', 'grp'), split_axis=0, concat_axis=0, tiled...  3.25 us
    pallas_call x1, Pallas kernels, send(): pl.pallas_call(functools.partial(pack_kernel, groups, chips, first, slots...  3.08 us
    pallas_call x1, Pallas kernels, match(): pl.pallas_call(functools.partial(match_own_kernel, chips, segments), out_...  2.91 us
    pallas_call x1, Pallas kernels, match(): pl.pallas_call(functools.partial(match_other_kernel, chips, segments, pat...  2.9 us
    all_to_all x1, waiting for transfers between devices, match(): lax.all_to_all(best, ('shard', 'grp'), split_axis=0, concat_axis=0, tiled...  2.74 us
    ppermute x2, starting transfers between devices, per_device(): past = jnp.maximum(past, lax.ppermute(past, axis, to))  2.16 us
    ppermute x2, waiting for transfers between devices, per_device(): past = jnp.maximum(past, lax.ppermute(past, axis, to))  2.02 us
  transfers between devices with their start and end apart: 4, of which 2 were waited for; matrix products, arithmetic and copies ran while one was open for 0% of the time, Pallas kernels for 9%

profile of v2, /device:TPU:0, one launch (start us, length us, event | category | flops | bytes accessed | tf_op | source)
XLA Modules:
  0.0 62.2 jit_solution(7924920563829870966)
XLA Ops:
  0.0 0.0 copy-start.6
  0.0 3.1 %pack.3 = (bf16[704,1024]{1,0:T(8,128)(2,1)S(1)}, s32[8,512]{1,0:T(8,128)S(1)}) custom-call(f32[512,1024]{1,0:T(8,128)} %emb_ref.1, s32[1,512]{1,0:T(1,128)} %bitcast.86, s32[1,512]{1,0:T(1,128)} %bitcast.88, s32[32,128]{1,0:T(8,128)} %bitcast.67), custom_call_target="tpu_custom_call" | custom-call | tf_op jit(solution)/shard_map/pack/pallas_call | solution.py:282
  3.1 41.6 %all_to_all.64 = bf16[8,88,1024]{2,1,0:T(8,128)(2,1)S(1)} all-to-all(bf16[8,88,1024]{2,1,0:T(8,128)(2,1)S(1)} %bitcast.62), channel_id=1, replica_groups=mesh['parts'=2,'shard'=4,'grp'=2,'sub'=2] {'shard','grp'}, dimensions={0} | all-to-all | bytes 2883584 | tf_op jit(solution)/shard_map/all_to_all | solution.py:298
  44.7 0.0 copy-start.2
  44.7 0.0 collective-permute-start.9
  44.7 0.6 collective-permute-start.7
  45.3 0.0 copy-done.6
  45.3 2.9 %match_own.3 = (f32[704,128]{1,0:T(8,128)S(1)}, f32[704,128]{1,0:T(8,128)S(1)}, bf16[704,128]{1,0:T(8,128)(2,1)S(1)}) custom-call(bf16[704,1024]{1,0:T(8,128)(2,1)S(1)} %bitcast.70, s32[4,4]{1,0:T(4,128)S(1)} %copy-done.6), custom_call_target="tpu_custom_call" | custom-call | flops 1015021568 | bytes 1441792 | tf_op jit(solution)/shard_map/match_own/pallas_call | solution.py:311
  48.2 0.0 copy-start
  48.2 0.0 copy-start.1
  48.2 0.0 copy-start.4
  48.3 0.0 copy-start.5
  48.3 0.0 collective-permute-done.9.other_ref
  48.3 2.9 %match_other.3 = f32[8,128]{1,0:T(8,128)} custom-call(bf16[704,1024]{1,0:T(8,128)(2,1)S(1)} %bitcast.71, bf16[704,1024]{1,0:T(8,128)(2,1)S(1)} %collective-permute-done.9.other_ref, f32[704,128]{1,0:T(8,128)S(1)} %get-tuple-element.85.before_ref, f32[704,128]{1,0:T(8,128)S(1)} %get-tuple-element.86.label_ref, bf16[704,128]{1,0:T(8,128)(2,1)S(1)} %get-tuple-element.87.terms_ref), custom_call_target="tpu_custom_call" | custom-call | flops 1015021568 | bytes 1441792 | tf_op jit(solution)/shard_map/match_other/pallas_call | solution.py:324
  51.2 0.0 copy-done.2
  51.2 3.2 %all-to-all-start.6 = ((f32[8,1,128]{2,1,0:T(1,128)}), f32[8,1,128]{2,1,0:T(1,128)S(1)}, u32[]{:S(2)}, u32[]{:S(2)}) async-start(f32[8,1,128]{2,1,0:T(1,128)} %bitcast.31), calls=%async_computation.6 | async-start | bytes 8192 | tf_op jit(solution)/shard_map/all_to_all | solution.py:333
  54.4 0.0 collective-permute-done.7
  54.5 1.6 %collective-permute-start.8 = (f32[1,128]{1,0:T(1,128)S(1)}, f32[1,128]{1,0:T(1,128)S(1)}, u32[]{:S(2)}, u32[]{:S(2)}) collective-permute-start(f32[1,128]{1,0:T(1,128)S(1)} %fusion.29), channel_id=1, source_target_pairs={{0,16},{16,0},{1,17},{17,1},{2,18},{18,2},{3,19},{19,3},{4,20},{20... | collective-permute-start | bytes 1544 | tf_op jit(solution)/shard_map/ppermute | solution.py:361
  56.1 2.0 %collective-permute-done.8 = f32[1,128]{1,0:T(1,128)S(1)} collective-permute-done((f32[1,128]{1,0:T(1,128)S(1)}, f32[1,128]{1,0:T(1,128)S(1)}, u32[]{:S(2)}, u32[]{:S(2)}) %collective-permute-start.8) | collective-permute-done | bytes 544 | tf_op jit(solution)/shard_map/ppermute | solution.py:361
  58.1 2.7 %all-to-all-done.6 = f32[8,1,128]{2,1,0:T(1,128)S(1)} async-done(((f32[8,1,128]{2,1,0:T(1,128)}), f32[8,1,128]{2,1,0:T(1,128)S(1)}, u32[]{:S(2)}, u32[]{:S(2)}) %all-to-all-start.6) | async-done | bytes 4128 | tf_op jit(solution)/shard_map/all_to_all | solution.py:333
  60.9 1.0 %unpack.3 = f32[1,512]{1,0:T(1,128)} custom-call(f32[8,128]{1,0:T(8,128)S(1)} %bitcast.64, s32[8,512]{1,0:T(8,128)S(1)} %get-tuple-element.88.slot_ref), custom_call_target="tpu_custom_call" | custom-call | tf_op jit(solution)/shard_map/unpack/pallas_call | solution.py:334
  61.8 0.0 copy-done
  61.8 0.0 copy-done.1
  61.8 0.0 copy-done.4
  61.8 0.0 copy-done.5
  61.8 0.2 conditional.2
  (4 shorter events, 0.0 us)
Async XLA Ops:
  0.0 45.3 %copy-start.6 = (s32[4,4]{1,0:T(4,128)S(1)}, s32[4,4]{1,0:T(4,128)}, u32[]{:S(2)}) copy-start(s32[4,4]{1,0:T(4,128)} %pattern_ref.1) | copy-start | bytes 196
  44.7 6.5 %copy-start.2 = (bf16[8,88,1024]{2,1,0:T(8,128)(2,1)}, bf16[8,88,1024]{2,1,0:T(8,128)(2,1)S(1)}, u32[]{:S(2)}) copy-start(bf16[8,88,1024]{2,1,0:T(8,128)(2,1)S(1)} %all_to_all.64) | copy-start | bytes 4325380
  44.7 3.6 %collective-permute-start.9 = (bf16[704,1024]{1,0:T(8,128)(2,1)S(1)}, bf16[704,1024]{1,0:T(8,128)(2,1)S(1)}, u32[]{:S(2)}, u32[]{:S(2)}) collective-permute-start(bf16[704,1024]{1,0:T(8,128)(2,1)S(1)} %bitcast.69), channel_id=1, source_target_pairs={{0,1},{1,0},{2,3},{3,2},{4,5},{5,4},{6,7},{7,6},{8,9},{9,8},{10,11... | collective-permute-start | bytes 4325384 | tf_op jit(solution)/shard_map/ppermute | solution.py:309
  44.7 9.7 %collective-permute-start.7 = (f32[1,128]{1,0:T(1,128)S(1)}, f32[1,128]{1,0:T(1,128)S(1)}, u32[]{:S(2)}, u32[]{:S(2)}) collective-permute-start(f32[1,128]{1,0:T(1,128)S(1)} %bitcast_convert_fusion), channel_id=1, source_target_pairs={{0,1},{1,0},{2,3},{3,2},{4,5},{5,4},{6,7},{7,6},{8,9},{9,8},{10,11... | collective-permute-start | bytes 1544 | tf_op jit(solution)/shard_map/ppermute | solution.py:361
  48.2 13.6 %copy-start = (s32[4096]{0:T(1024)S(1)}, s32[4096]{0:T(1024)}, u32[]{:S(2)}) copy-start(s32[4096]{0:T(1024)} %param.12) | copy-start | bytes 49156
  48.2 13.6 %copy-start.1 = (f32[512,1024]{1,0:T(8,128)S(1)}, f32[512,1024]{1,0:T(8,128)}, u32[]{:S(2)}) copy-start(f32[512,1024]{1,0:T(8,128)} %emb_ref.1) | copy-start | bytes 6291460
  48.2 13.6 %copy-start.4 = (s32[512]{0:T(512)S(1)}, s32[512]{0:T(512)}, u32[]{:S(2)}) copy-start(s32[512]{0:T(512)} %param.10) | copy-start | bytes 6148
  48.3 13.6 %copy-start.5 = (s32[512]{0:T(512)S(1)}, s32[512]{0:T(512)}, u32[]{:S(2)}) copy-start(s32[512]{0:T(512)} %param.11) | copy-start | bytes 6148
  51.2 9.7 %all-to-all-start.6 = ((f32[8,1,128]{2,1,0:T(1,128)}), f32[8,1,128]{2,1,0:T(1,128)S(1)}, u32[]{:S(2)}, u32[]{:S(2)}) async-start(f32[8,1,128]{2,1,0:T(1,128)} %bitcast.31), calls=%async_computation.6 | async-start | bytes 8192 | tf_op jit(solution)/shard_map/all_to_all | solution.py:333
  54.5 3.6 %collective-permute-start.8 = (f32[1,128]{1,0:T(1,128)S(1)}, f32[1,128]{1,0:T(1,128)S(1)}, u32[]{:S(2)}, u32[]{:S(2)}) collective-permute-start(f32[1,128]{1,0:T(1,128)S(1)} %fusion.29), channel_id=1, source_target_pairs={{0,16},{16,0},{1,17},{17,1},{2,18},{18,2},{3,19},{19,3},{4,20},{20... | collective-permute-start | bytes 1544 | tf_op jit(solution)/shard_map/ppermute | solution.py:361

commit v3 on v2

--- a/solution.py
+++ b/solution.py
@@ -10,10 +10,10 @@
 
 BF16 = jnp.bfloat16
 F32 = jnp.float32
-VMEM_LIMIT = 48 * 1024 * 1024
+VMEM_LIMIT = 32 * 1024 * 1024
 LANES = 128
-MORE = 40
-BARRED = 4.0
+PIECES = 2
+MORE = (16, 40)
 
 
 def row_masks(doc_codes, pattern):
@@ -90,9 +90,24 @@
 
 
 def pack_kernel(
-    groups, chips, first, slots, count, emb_ref, label_ref, block_ref, assign_ref, out_ref, slot_ref
+    groups, chips, first, slots, count, emb_hbm, label_hbm, block_hbm, assign_hbm, out_ref,
+    slot_ref, emb_ref, label_ref, block_ref, assign_ref, unit_ref, copied,
 ):
-    docs, features = emb_ref.shape
+    docs, features = emb_hbm.shape
+    step = docs // PIECES
+    small = [(label_hbm, label_ref), (assign_hbm, assign_ref), (block_hbm, block_ref)]
+    moves = list(small)
+    for piece in range(PIECES):
+        rows = pl.ds(piece * step, step)
+        moves.append((emb_hbm.at[rows], emb_ref.at[rows]))
+    copies = [
+        pltpu.make_async_copy(source, target, copied.at[i])
+        for i, (source, target) in enumerate(moves)
+    ]
+    for copy in copies:
+        copy.start()
+    for copy in copies[: len(small)]:
+        copy.wait()
     labels = label_ref[...]
     clusters = assign_ref.shape[0] * assign_ref.shape[1]
     assign = assign_ref[...]
@@ -127,11 +142,13 @@
     ).astype(jnp.int32) - first
     most = jnp.max(jnp.where(member, rank, -1), axis=0, keepdims=True)
     most = jnp.max(most, axis=1, keepdims=True)
-    past = jnp.where(most >= slots - 1, 1.0, 0.0) + jnp.where(most >= slots + MORE - 2, 1.0, 0.0)
+    past = jnp.where(most >= slots - 1, 1.0, 0.0)
+    for more in MORE:
+        past = past + jnp.where(most >= slots + more - 2, 1.0, 0.0)
     slot = jnp.where(member & (rank >= 0) & (rank < slots - 1), rank, -1)
     slot_ref[...] = slot
 
-    code = (labels + group) * count + block_ref[...] + 1
+    code = (labels + group + 2) * count + block_ref[...] + 1
     row_id = lax.broadcasted_iota(jnp.int32, (8, docs), 0)
     digits = jnp.where(row_id == 0, code >> 7, jnp.where(row_id == 1, code & 127, 0))
     digits = digits.astype(F32).astype(BF16)
@@ -139,109 +156,97 @@
     slot_id = lax.broadcasted_iota(jnp.int32, (chips, slots, docs), 1)
     picks = (slot_id == slot[:, None, :]).astype(F32).reshape(chips * slots, docs).astype(BF16)
 
-    lane_slot = lax.broadcasted_iota(jnp.int32, (LANES, docs), 0)
-    code_rows = []
+    sent = dot_nt(digits, picks)
+    tail = lax.broadcasted_iota(jnp.int32, (8, 3 * LANES), 0) == 7
+    fill = jnp.zeros((1, LANES - slots), F32)
+    for piece, copy in enumerate(copies[len(small) :]):
+        copy.wait()
+        rows = slice(piece * step, (piece + 1) * step)
+        emb = emb_ref[rows, :]
+        scale = lax.rsqrt(jnp.sum(emb * emb, axis=1, keepdims=True) + 1e-06)
+        unit_ref[rows, :] = (emb * scale).astype(BF16)
+    step = min(features, 4 * LANES)
+    for at in range(0, features, step):
+        rows = jnp.dot(picks, unit_ref[:, at : at + step], preferred_element_type=F32)
+        out_ref[:, at : at + step] = rows.astype(BF16)
     for chip in range(chips):
-        pick = (lane_slot == slot[chip : chip + 1, :]).astype(F32).astype(BF16)
-        sent = dot_nt(digits, pick)
-        row = [sent[0:1, :], sent[1:2, :], jnp.broadcast_to(past, (1, LANES))]
-        row.append(jnp.zeros((1, features - 3 * LANES), F32))
-        code_rows.append(jnp.concatenate(row, axis=1))
-    code_rows = jnp.concatenate(code_rows, axis=0)
-
-    emb = emb_ref[...]
-    unit = (emb * lax.rsqrt(jnp.sum(emb * emb, axis=1, keepdims=True) + 1e-06)).astype(BF16)
-    step = min(features, 4 * LANES)
-    last = lax.broadcasted_iota(jnp.int32, (chips, slots, step), 1) == slots - 1
-    for at in range(0, features, step):
-        rows = jnp.dot(picks, unit[:, at : at + step], preferred_element_type=F32)
-        rows = rows.reshape(chips, slots, step)
-        rows = jnp.where(last, code_rows[:, None, at : at + step], rows)
-        out_ref[:, at : at + step] = rows.reshape(chips * slots, step).astype(BF16)
-
-
-def codes_of(rows_ref, chips, segments, count):
-    rows = rows_ref.shape[0]
+        here = slice(chip * slots, (chip + 1) * slots)
+        row = [sent[0:1, here], fill, sent[1:2, here], fill, jnp.broadcast_to(past, (1, LANES))]
+        end = (chip + 1) * slots
+        held = out_ref[end - 8 : end, : 3 * LANES].astype(F32)
+        held = jnp.where(tail, jnp.concatenate(row, axis=1), held)
+        out_ref[end - 8 : end, : 3 * LANES] = held.astype(BF16)
+
+
+def codes_of(rows_ref, chips, segments):
     slots = sum(segments)
-    at_row = lax.broadcasted_iota(jnp.int32, (chips, rows), 1)
-    chip_row = lax.broadcasted_iota(jnp.int32, (chips, rows), 0) * slots
-    found, begin = [], 0
-    for length in segments:
-        pick = (at_row == chip_row + (begin + length - 1)).astype(F32).astype(BF16)
-        sent = jnp.dot(pick, rows_ref[:, : 2 * LANES], preferred_element_type=F32)
-        found.append(sent[:, :LANES] * 128.0 + sent[:, LANES:])
-        begin += length
     pieces = []
     for chip in range(chips):
-        for length, code in zip(segments, found):
-            pieces.append(code[chip : chip + 1, :length])
-    code = jnp.concatenate(pieces, axis=1) - 1.0
-    label = jnp.floor((code + 0.5) / count)
-    block = jnp.where(code < 0.0, -1.0, code - label * count)
-    return jnp.where(code < 0.0, -8.0, label), block
-
-
-def down(row):
-    return jnp.transpose(jnp.broadcast_to(row, (8, row.shape[1])))[:, 0:1]
-
-
-def hot_blocks(block):
-    lane = lax.broadcasted_iota(jnp.int32, (block.shape[0], LANES), 1).astype(F32)
-    return (lane == block).astype(F32).astype(BF16)
-
-
-def match_rows(left_ref, row_label, row_terms, right_ref, label, hot, same, best):
+        end = chip * slots
+        for length in segments:
+            end += length
+            sent = rows_ref[end - 8 : end, : 2 * LANES].astype(F32)[7:8, :]
+            pieces.append((sent[:, :LANES] * 128.0 + sent[:, LANES:])[:, :length])
+    return jnp.concatenate(pieces, axis=1).astype(jnp.int32)
+
+
+def match_rows(left_ref, row_base, row_bits, right_ref, code, same, best):
     rows, columns = left_ref.shape[0], right_ref.shape[0]
-    row_at = lax.broadcasted_iota(jnp.int32, (rows, LANES), 0)
-    col_at = lax.broadcasted_iota(jnp.int32, (rows, LANES), 1)
+    apart = lax.broadcasted_iota(jnp.int32, (rows, LANES), 0) - lax.broadcasted_iota(
+        jnp.int32, (rows, LANES), 1
+    )
     left = left_ref[...]
     step = 2 * LANES
     for at in range(0, columns, step):
         width = min(step, columns - at)
         sim = dot_nt(left, right_ref[at : at + width, :])
-        sim += dot_nt(row_terms, hot[at : at + width, :])
         for piece in range(0, width, LANES):
             span = min(LANES, width - piece)
-            near = jnp.abs(row_label[:, :span] - label[:, at + piece : at + piece + span]) <= 1.0
+            begin = at + piece
+            gap = code[:, begin : begin + span] - row_base[:, :span]
+            gap = jnp.minimum(jnp.maximum(gap, 0), 31)
+            fits = jnp.left_shift(row_bits[:, :span], gap) < 0
             if same:
-                near = near & (row_at[:, :span] != col_at[:, :span] + (at + piece))
-            value = jnp.where(near, sim[:, piece : piece + span], -1.0)
+                fits = fits & (apart[:, :span] != begin)
+            value = jnp.where(fits, sim[:, piece : piece + span], -1.0)
             if span < LANES:
                 value = jnp.concatenate([value, jnp.full((rows, LANES - span), -1.0, F32)], axis=1)
             best = jnp.maximum(best, value)
     return best
 
 
-def match_own_kernel(
-    chips, segments, own_ref, pattern_ref, best_ref, label_ref, terms_ref
-):
+def match_own_kernel(chips, segments, own_ref, pattern_ref, best_ref, base_ref, bits_ref):
     rows = own_ref.shape[0]
     count = pattern_ref.shape[0]
-    label, block = codes_of(own_ref, chips, segments, count)
-    hot = hot_blocks(down(block))
-    table = jnp.zeros((LANES, LANES), F32)
-    from_block = lax.broadcasted_iota(jnp.int32, (LANES, LANES), 0)
-    to_block = lax.broadcasted_iota(jnp.int32, (LANES, LANES), 1)
+    code = codes_of(own_ref, chips, segments)
+    label = jnp.floor((code.astype(F32) - 0.5) / count).astype(jnp.int32)
+    block = code - 1 - label * count
+    base = count * (label - 1)
+    bits = jnp.zeros_like(code)
     for a in range(count):
+        word = 0
         for b in range(count):
-            term = BARRED * (pattern_ref[a, b].astype(F32) - 1.0)
-            table = jnp.where((from_block == a) & (to_block == b), term, table)
-    row_terms = jnp.dot(hot, table.astype(BF16), preferred_element_type=F32).astype(BF16)
-    row_label = jnp.broadcast_to(down(label), (rows, LANES))
-    label_ref[...] = row_label
-    terms_ref[...] = row_terms
+            for turn in range(3):
+                word += pattern_ref[a, b] << (30 - turn * count - b)
+        bits = jnp.where(block == a, word, bits)
+    bits = jnp.where(code == 0, 0, bits)
+    both = jnp.concatenate([base, bits, jnp.zeros((6, rows), jnp.int32)], axis=0)
+    both = jnp.transpose(both)
+    row_base = jnp.broadcast_to(both[:, 0:1], (rows, LANES))
+    row_bits = jnp.broadcast_to(both[:, 1:2], (rows, LANES))
+    base_ref[...] = row_base
+    bits_ref[...] = row_bits
     best = jnp.full((rows, LANES), -1.0, F32)
-    best_ref[...] = match_rows(own_ref, row_label, row_terms, own_ref, label, hot, True, best)
+    best_ref[...] = match_rows(own_ref, row_base, row_bits, own_ref, code, True, best)
 
 
 def match_other_kernel(
-    chips, segments, count, own_ref, other_ref, before_ref, label_ref, terms_ref, best_ref
+    chips, segments, own_ref, other_ref, before_ref, base_ref, bits_ref, best_ref
 ):
     slots = sum(segments)
-    label, block = codes_of(other_ref, chips, segments, count)
-    hot = hot_blocks(down(block))
+    code = codes_of(other_ref, chips, segments)
     best = match_rows(
-        own_ref, label_ref[...], terms_ref[...], other_ref, label, hot, False, before_ref[...]
+        own_ref, base_ref[...], bits_ref[...], other_ref, code, False, before_ref[...]
     )
     across = jnp.max(jnp.transpose(best), axis=0, keepdims=True)
     for chip in range(chips):
@@ -285,8 +290,16 @@
             jax.ShapeDtypeStruct((chips * slots, features), BF16),
             jax.ShapeDtypeStruct((chips, docs), jnp.int32),
         ),
-        in_specs=[in_vmem()] * 4,
+        in_specs=[pl.BlockSpec(memory_space=pl.ANY)] * 4,
         out_specs=(in_vmem(), in_vmem()),
+        scratch_shapes=[
+            pltpu.VMEM((docs, features), F32),
+            pltpu.VMEM((1, docs), jnp.int32),
+            pltpu.VMEM((1, docs), jnp.int32),
+            pltpu.VMEM((assign.shape[0] // LANES, LANES), jnp.int32),
+            pltpu.VMEM((docs, features), BF16),
+            pltpu.SemaphoreType.DMA((3 + PIECES,)),
+        ],
         compiler_params=params(),
         name="pack",
     )(
@@ -308,12 +321,12 @@
     cores = lax.axis_size("sub")
     other = lax.ppermute(arrived, "sub", [(i, (i + 1) % cores) for i in range(cores)])
     work = cost(2 * rows * rows * features, 2 * rows * features)
-    best, label, terms = pl.pallas_call(
+    best, base, bits = pl.pallas_call(
         functools.partial(match_own_kernel, chips, segments),
         out_shape=(
             jax.ShapeDtypeStruct((rows, LANES), F32),
-            jax.ShapeDtypeStruct((rows, LANES), F32),
-            jax.ShapeDtypeStruct((rows, LANES), BF16),
+            jax.ShapeDtypeStruct((rows, LANES), jnp.int32),
+            jax.ShapeDtypeStruct((rows, LANES), jnp.int32),
         ),
         in_specs=[in_vmem(), in_smem()],
         out_specs=(in_vmem(), in_vmem(), in_vmem()),
@@ -322,14 +335,14 @@
         name="match_own",
     )(arrived, pattern)
     best = pl.pallas_call(
-        functools.partial(match_other_kernel, chips, segments, pattern.shape[0]),
+        functools.partial(match_other_kernel, chips, segments),
         out_shape=jax.ShapeDtypeStruct((chips, LANES), F32),
         in_specs=[in_vmem()] * 5,
         out_specs=in_vmem(),
         compiler_params=params(),
         cost_estimate=work,
         name="match_other",
-    )(arrived, other, best, label, terms)
+    )(arrived, other, best, base, bits)
     back = lax.all_to_all(best, ("shard", "grp"), split_axis=0, concat_axis=0, tiled=True)
     return pl.pallas_call(
         functools.partial(unpack_kernel, chips, slots),
@@ -360,21 +373,24 @@
             to = [(i, (i + shift) % size) for i in range(size)]
             past = jnp.maximum(past, lax.ppermute(past, axis, to))
 
-    def second_round():
-        more, more_slot = send(*inputs, count, slots - 1, MORE)
+    def second_round(size):
+        more, more_slot = send(*inputs, count, slots - 1, size)
         both = jnp.concatenate(
-            [arrived.reshape(chips, slots, features), more.reshape(chips, MORE, features)], axis=1
-        ).reshape(chips * (slots + MORE), features)
+            [arrived.reshape(chips, slots, features), more.reshape(chips, size, features)], axis=1
+        ).reshape(chips * (slots + size), features)
         both_slot = jnp.where(more_slot >= 0, more_slot + slots, slot)
-        return match(both, both_slot, pattern, (slots, MORE))
-
-    return lax.cond(
-        past[0, 0] > 0.0,
-        lambda: lax.cond(
-            past[0, 0] > 1.0, lambda: general_form(*inputs, pattern), second_round
-        ),
-        lambda: found,
-    )
+        return match(both, both_slot, pattern, (slots, size))
+
+    def in_rounds(level):
+        if level > len(MORE):
+            return general_form(*inputs, pattern)
+        return lax.cond(
+            past[0, 0] > level,
+            lambda: in_rounds(level + 1),
+            lambda: second_round(MORE[level - 1]) if level else found,
+        )
+
+    return in_rounds(0)
 
 
 def solution(mesh):

time: 62.5 us -> 61 us (0.976)
  Pallas kernels: 9.84 us -> 7.87 us
    pallas_call x1, Pallas kernels: 2.91 us -> 2.04 us  [match(): pl.pallas_call(functools.partial(match_own_kernel, chips, segments), out_...]
  transfers between devices with their start and end apart: 4 -> 4, of which waited for: 2 -> 3; matrix products, arithmetic and copies ran while one was open for 0% -> 0% of each run, Pallas kernels for 9% -> 7%
where the time goes in v3:
time: 61 us; the launch traced here: 60.8 us
  blocking collectives  41.6 us (68%)
  Pallas kernels  7.87 us (13%)
  starting transfers between devices  5.42 us (9%)
  waiting for transfers between devices  5.27 us (9%)
    all_to_all x1, blocking collectives, send(): lax.all_to_all(outgoing, ('shard', 'grp'), split_axis=0, concat_axis=0, t...  41.6 us
    all_to_all x1, starting transfers between devices, match(): lax.all_to_all(best, ('shard', 'grp'), split_axis=0, concat_axis=0, tiled...  3.27 us
    all_to_all x1, waiting for transfers between devices, match(): lax.all_to_all(best, ('shard', 'grp'), split_axis=0, concat_axis=0, tiled...  2.72 us
    pallas_call x1, Pallas kernels, send(): pl.pallas_call(functools.partial(pack_kernel, groups, chips, first, slots...  2.59 us
    pallas_call x1, Pallas kernels, match(): pl.pallas_call(functools.partial(match_other_kernel, chips, segments), ou...  2.29 us
    ppermute x2, starting transfers between devices, per_device(): past = jnp.maximum(past, lax.ppermute(past, axis, to))  2.15 us
    pallas_call x1, Pallas kernels, match(): pl.pallas_call(functools.partial(match_own_kernel, chips, segments), out_...  2.04 us
    ppermute x2, waiting for transfers between devices, per_device(): past = jnp.maximum(past, lax.ppermute(past, axis, to))  2.03 us
  transfers between devices with their start and end apart: 4, of which 3 were waited for; matrix products, arithmetic and copies ran while one was open for 0% of the time, Pallas kernels for 7%

profile of v3, /device:TPU:0, one launch (start us, length us, event | category | flops | bytes accessed | tf_op | source)
XLA Modules:
  0.0 60.8 jit_solution(2985241541803120555)
XLA Ops:
  0.0 0.0 copy-start.7
  0.0 2.6 %pack.5 = (bf16[704,1024]{1,0:T(8,128)(2,1)S(1)}, s32[8,512]{1,0:T(8,128)S(1)}) custom-call(f32[512,1024]{1,0:T(8,128)} %emb_hbm.1, s32[1,512]{1,0:T(1,128)} %bitcast.106, s32[1,512]{1,0:T(1,128)} %bitcast.109, s32[32,128]{1,0:T(8,128)} %bitcast.85), custom_call_target="tpu_custom_call" | custom-call | tf_op jit(solution)/shard_map/pack/pallas_call | solution.py:287
  2.6 41.6 %all_to_all.80 = bf16[8,88,1024]{2,1,0:T(8,128)(2,1)S(1)} all-to-all(bf16[8,88,1024]{2,1,0:T(8,128)(2,1)S(1)} %bitcast.78), channel_id=1, replica_groups=mesh['parts'=2,'shard'=4,'grp'=2,'sub'=2] {'shard','grp'}, dimensions={0} | all-to-all | bytes 2883584 | tf_op jit(solution)/shard_map/all_to_all | solution.py:311
  44.2 0.0 copy-start.2
  44.2 0.0 collective-permute-start.10
  44.3 0.6 collective-permute-start.8
  44.8 0.0 copy-done.7
  44.8 2.0 %match_own.5 = (f32[704,128]{1,0:T(8,128)S(1)}, s32[704,128]{1,0:T(8,128)S(1)}, s32[704,128]{1,0:T(8,128)S(1)}) custom-call(bf16[704,1024]{1,0:T(8,128)(2,1)S(1)} %bitcast.89, s32[4,4]{1,0:T(4,128)S(1)} %copy-done.7), custom_call_target="tpu_custom_call" | custom-call | flops 1015021568 | bytes 1441792 | tf_op jit(solution)/shard_map/match_own/pallas_call | solution.py:324
  46.9 0.0 copy-start
  46.9 0.0 copy-start.1
  46.9 0.0 copy-start.5
  46.9 0.0 copy-start.6
  46.9 0.5 collective-permute-done.10.other_ref
  47.4 2.3 %match_other.5 = f32[8,128]{1,0:T(8,128)} custom-call(bf16[704,1024]{1,0:T(8,128)(2,1)S(1)} %bitcast.90, bf16[704,1024]{1,0:T(8,128)(2,1)S(1)} %collective-permute-done.10.other_ref, f32[704,128]{1,0:T(8,128)S(1)} %get-tuple-element.138.before_ref, s32[704,128]{1,0:T(8,128)S(1)} %get-tuple-element.139.base_ref, s32[704,128]{1,0:T(8,128)S(1)} %get-tuple-element.140.bits_ref), custom_call_target="tpu_custom_call" | custom-call | flops 1015021568 | bytes 1441792 | tf_op jit(solution)/shard_map/match_other/pallas_call | solution.py:337
  49.7 0.0 copy-done.2
  49.7 3.3 %all-to-all-start.8 = ((f32[8,1,128]{2,1,0:T(1,128)}), f32[8,1,128]{2,1,0:T(1,128)S(1)}, u32[]{:S(2)}, u32[]{:S(2)}) async-start(f32[8,1,128]{2,1,0:T(1,128)} %bitcast.42), calls=%async_computation.8 | async-start | bytes 8192 | tf_op jit(solution)/shard_map/all_to_all | solution.py:346
  53.0 0.0 collective-permute-done.8
  53.0 1.6 %collective-permute-start.9 = (f32[1,128]{1,0:T(1,128)S(1)}, f32[1,128]{1,0:T(1,128)S(1)}, u32[]{:S(2)}, u32[]{:S(2)}) collective-permute-start(f32[1,128]{1,0:T(1,128)S(1)} %fusion.29), channel_id=1, source_target_pairs={{0,16},{16,0},{1,17},{17,1},{2,18},{18,2},{3,19},{19,3},{4,20},{20... | collective-permute-start | bytes 1544 | tf_op jit(solution)/shard_map/ppermute | solution.py:374
  54.6 2.0 %collective-permute-done.9 = f32[1,128]{1,0:T(1,128)S(1)} collective-permute-done((f32[1,128]{1,0:T(1,128)S(1)}, f32[1,128]{1,0:T(1,128)S(1)}, u32[]{:S(2)}, u32[]{:S(2)}) %collective-permute-start.9) | collective-permute-done | bytes 544 | tf_op jit(solution)/shard_map/ppermute | solution.py:374
  56.7 2.7 %all-to-all-done.8 = f32[8,1,128]{2,1,0:T(1,128)S(1)} async-done(((f32[8,1,128]{2,1,0:T(1,128)}), f32[8,1,128]{2,1,0:T(1,128)S(1)}, u32[]{:S(2)}, u32[]{:S(2)}) %all-to-all-start.8) | async-done | bytes 4128 | tf_op jit(solution)/shard_map/all_to_all | solution.py:346
  59.4 1.0 %unpack.5 = f32[1,512]{1,0:T(1,128)} custom-call(f32[8,128]{1,0:T(8,128)S(1)} %bitcast.81, s32[8,512]{1,0:T(8,128)S(1)} %get-tuple-element.141.slot_ref), custom_call_target="tpu_custom_call" | custom-call | tf_op jit(solution)/shard_map/unpack/pallas_call | solution.py:347
  60.4 0.0 copy-done
  60.4 0.0 copy-done.1
  60.4 0.0 copy-done.5
  60.4 0.0 copy-done.6
  60.4 0.2 conditional.3
  (4 shorter events, 0.0 us)
Async XLA Ops:
  0.0 44.8 %copy-start.7 = (s32[4,4]{1,0:T(4,128)S(1)}, s32[4,4]{1,0:T(4,128)}, u32[]{:S(2)}) copy-start(s32[4,4]{1,0:T(4,128)} %pattern_ref.1) | copy-start | bytes 196
  44.2 5.5 %copy-start.2 = (bf16[8,88,1024]{2,1,0:T(8,128)(2,1)}, bf16[8,88,1024]{2,1,0:T(8,128)(2,1)S(1)}, u32[]{:S(2)}) copy-start(bf16[8,88,1024]{2,1,0:T(8,128)(2,1)S(1)} %all_to_all.80) | copy-start | bytes 4325380
  44.2 3.2 %collective-permute-start.10 = (bf16[704,1024]{1,0:T(8,128)(2,1)S(1)}, bf16[704,1024]{1,0:T(8,128)(2,1)S(1)}, u32[]{:S(2)}, u32[]{:S(2)}) collective-permute-start(bf16[704,1024]{1,0:T(8,128)(2,1)S(1)} %bitcast.88), channel_id=1, source_target_pairs={{0,1},{1,0},{2,3},{3,2},{4,5},{5,4},{6,7},{7,6},{8,9},{9,8},{10,11... | collective-permute-start | bytes 4325384 | tf_op jit(solution)/shard_map/ppermute | solution.py:322
  44.3 8.8 %collective-permute-start.8 = (f32[1,128]{1,0:T(1,128)S(1)}, f32[1,128]{1,0:T(1,128)S(1)}, u32[]{:S(2)}, u32[]{:S(2)}) collective-permute-start(f32[1,128]{1,0:T(1,128)S(1)} %bitcast_convert_fusion), channel_id=1, source_target_pairs={{0,1},{1,0},{2,3},{3,2},{4,5},{5,4},{6,7},{7,6},{8,9},{9,8},{10,11... | collective-permute-start | bytes 1544 | tf_op jit(solution)/shard_map/ppermute | solution.py:374
  46.9 13.5 %copy-start = (s32[4096]{0:T(1024)S(1)}, s32[4096]{0:T(1024)}, u32[]{:S(2)}) copy-start(s32[4096]{0:T(1024)} %param.14) | copy-start | bytes 49156
  46.9 13.5 %copy-start.1 = (f32[512,1024]{1,0:T(8,128)S(1)}, f32[512,1024]{1,0:T(8,128)}, u32[]{:S(2)}) copy-start(f32[512,1024]{1,0:T(8,128)} %emb_hbm.1) | copy-start | bytes 6291460
  46.9 13.5 %copy-start.5 = (s32[512]{0:T(512)S(1)}, s32[512]{0:T(512)}, u32[]{:S(2)}) copy-start(s32[512]{0:T(512)} %param.12) | copy-start | bytes 6148
  46.9 13.5 %copy-start.6 = (s32[512]{0:T(512)S(1)}, s32[512]{0:T(512)}, u32[]{:S(2)}) copy-start(s32[512]{0:T(512)} %param.13) | copy-start | bytes 6148
  49.7 9.7 %all-to-all-start.8 = ((f32[8,1,128]{2,1,0:T(1,128)}), f32[8,1,128]{2,1,0:T(1,128)S(1)}, u32[]{:S(2)}, u32[]{:S(2)}) async-start(f32[8,1,128]{2,1,0:T(1,128)} %bitcast.42), calls=%async_computation.8 | async-start | bytes 8192 | tf_op jit(solution)/shard_map/all_to_all | solution.py:346
  53.0 3.6 %collective-permute-start.9 = (f32[1,128]{1,0:T(1,128)S(1)}, f32[1,128]{1,0:T(1,128)S(1)}, u32[]{:S(2)}, u32[]{:S(2)}) collective-permute-start(f32[1,128]{1,0:T(1,128)S(1)} %fusion.29), channel_id=1, source_target_pairs={{0,16},{16,0},{1,17},{17,1},{2,18},{18,2},{3,19},{19,3},{4,20},{20... | collective-permute-start | bytes 1544 | tf_op jit(solution)/shard_map/ppermute | solution.py:374

commit v4 on v3

--- a/solution.py
+++ b/solution.py
@@ -13,7 +13,7 @@
 VMEM_LIMIT = 32 * 1024 * 1024
 LANES = 128
 PIECES = 2
-MORE = (16, 40)
+MORE = (24, 40)
 
 
 def row_masks(doc_codes, pattern):
@@ -178,16 +178,31 @@
         out_ref[end - 8 : end, : 3 * LANES] = held.astype(BF16)
 
 
-def codes_of(rows_ref, chips, segments):
-    slots = sum(segments)
+def codes_of(rows_ref, chips):
+    slots = rows_ref.shape[0] // chips
     pieces = []
-    for chip in range(chips):
-        end = chip * slots
-        for length in segments:
-            end += length
-            sent = rows_ref[end - 8 : end, : 2 * LANES].astype(F32)[7:8, :]
-            pieces.append((sent[:, :LANES] * 128.0 + sent[:, LANES:])[:, :length])
+    for end in range(slots, chips * slots + 1, slots):
+        sent = rows_ref[end - 8 : end, : 2 * LANES].astype(F32)[7:8, :]
+        pieces.append((sent[:, :LANES] * 128.0 + sent[:, LANES:])[:, :slots])
     return jnp.concatenate(pieces, axis=1).astype(jnp.int32)
+
+
+def row_words(code, pattern_ref):
+    rows = code.shape[1]
+    count = pattern_ref.shape[0]
+    label = jnp.floor((code.astype(F32) - 0.5) / count).astype(jnp.int32)
+    block = code - 1 - label * count
+    base = count * (label - 1)
+    bits = jnp.zeros_like(code)
+    for a in range(count):
+        word = 0
+        for b in range(count):
+            for turn in range(3):
+                word += pattern_ref[a, b] << (30 - turn * count - b)
+        bits = jnp.where(block == a, word, bits)
+    bits = jnp.where(code == 0, 0, bits)
+    both = jnp.transpose(jnp.concatenate([base, bits, jnp.zeros((6, rows), jnp.int32)], axis=0))
+    return tuple(jnp.broadcast_to(both[:, i : i + 1], (rows, LANES)) for i in range(2))
 
 
 def match_rows(left_ref, row_base, row_bits, right_ref, code, same, best):
@@ -215,45 +230,58 @@
     return best
 
 
-def match_own_kernel(chips, segments, own_ref, pattern_ref, best_ref, base_ref, bits_ref):
-    rows = own_ref.shape[0]
-    count = pattern_ref.shape[0]
-    code = codes_of(own_ref, chips, segments)
-    label = jnp.floor((code.astype(F32) - 0.5) / count).astype(jnp.int32)
-    block = code - 1 - label * count
-    base = count * (label - 1)
-    bits = jnp.zeros_like(code)
-    for a in range(count):
-        word = 0
-        for b in range(count):
-            for turn in range(3):
-                word += pattern_ref[a, b] << (30 - turn * count - b)
-        bits = jnp.where(block == a, word, bits)
-    bits = jnp.where(code == 0, 0, bits)
-    both = jnp.concatenate([base, bits, jnp.zeros((6, rows), jnp.int32)], axis=0)
-    both = jnp.transpose(both)
-    row_base = jnp.broadcast_to(both[:, 0:1], (rows, LANES))
-    row_bits = jnp.broadcast_to(both[:, 1:2], (rows, LANES))
-    base_ref[...] = row_base
-    bits_ref[...] = row_bits
-    best = jnp.full((rows, LANES), -1.0, F32)
-    best_ref[...] = match_rows(own_ref, row_base, row_bits, own_ref, code, True, best)
+def match_own_kernel(chips, own_ref, pattern_ref, best_ref, base_ref, bits_ref):
+    code = codes_of(own_ref, chips)
+    base, bits = row_words(code, pattern_ref)
+    base_ref[...] = base
+    bits_ref[...] = bits
+    best = jnp.full(base.shape, -1.0, F32)
+    best_ref[...] = match_rows(own_ref, base, bits, own_ref, code, True, best)
+
+
+def by_chip(best, chips):
+    across = jnp.max(jnp.transpose(best), axis=0, keepdims=True)
+    slots = across.shape[1] // chips
+    return [across[:, chip * slots : (chip + 1) * slots] for chip in range(chips)]
 
 
 def match_other_kernel(
-    chips, segments, own_ref, other_ref, before_ref, base_ref, bits_ref, best_ref
+    chips, own_ref, other_ref, before_ref, base_ref, bits_ref, best_ref
 ):
-    slots = sum(segments)
-    code = codes_of(other_ref, chips, segments)
+    slots = own_ref.shape[0] // chips
+    code = codes_of(other_ref, chips)
     best = match_rows(
         own_ref, base_ref[...], bits_ref[...], other_ref, code, False, before_ref[...]
     )
-    across = jnp.max(jnp.transpose(best), axis=0, keepdims=True)
-    for chip in range(chips):
-        best_ref[chip : chip + 1, 0:slots] = across[:, chip * slots : (chip + 1) * slots]
-
-
-def unpack_kernel(chips, slots, back_ref, slot_ref, out_ref):
+    for chip, found in enumerate(by_chip(best, chips)):
+        best_ref[chip : chip + 1, 0:slots] = found
+
+
+def match_more_kernel(
+    chips, own_ref, other_ref, more_ref, more_other_ref, base_ref, bits_ref, pattern_ref,
+    before_ref, best_ref,
+):
+    slots, size = own_ref.shape[0] // chips, more_ref.shape[0] // chips
+    code, code_other = codes_of(more_ref, chips), codes_of(more_other_ref, chips)
+    best = jnp.full((chips * slots, LANES), -1.0, F32)
+    base, bits = base_ref[...], bits_ref[...]
+    best = match_rows(own_ref, base, bits, more_ref, code, False, best)
+    best = match_rows(own_ref, base, bits, more_other_ref, code_other, False, best)
+    for chip, found in enumerate(by_chip(best, chips)):
+        here = slice(chip, chip + 1)
+        best_ref[here, 0:slots] = jnp.maximum(before_ref[here, 0:slots], found)
+
+    base, bits = row_words(code, pattern_ref)
+    best = jnp.full((chips * size, LANES), -1.0, F32)
+    best = match_rows(more_ref, base, bits, own_ref, codes_of(own_ref, chips), False, best)
+    best = match_rows(more_ref, base, bits, other_ref, codes_of(other_ref, chips), False, best)
+    best = match_rows(more_ref, base, bits, more_ref, code, True, best)
+    best = match_rows(more_ref, base, bits, more_other_ref, code_other, False, best)
+    for chip, found in enumerate(by_chip(best, chips)):
+        best_ref[chip : chip + 1, slots : slots + size] = found
+
+
+def unpack_kernel(chips, slots, back_ref, slot_ref, direct_ref, out_ref):
     docs = slot_ref.shape[1]
     back = jnp.transpose(back_ref[...])
     slot_id = lax.broadcasted_iota(jnp.int32, (slots, docs), 0)
@@ -261,7 +289,7 @@
     for chip in range(chips):
         here = slot_id == slot_ref[chip : chip + 1, :]
         best = jnp.maximum(best, jnp.where(here, back[0:slots, chip : chip + 1], -1.0))
-    out_ref[...] = jnp.max(best, axis=0, keepdims=True)
+    out_ref[...] = jnp.maximum(jnp.max(best, axis=0, keepdims=True), direct_ref[...])
 
 
 def in_vmem():
@@ -314,15 +342,28 @@
     return arrived, slot
 
 
-def match(arrived, slot, pattern, segments):
-    chips, docs = slot.shape
-    slots = sum(segments)
-    rows, features = arrived.shape
+def swap(rows):
     cores = lax.axis_size("sub")
-    other = lax.ppermute(arrived, "sub", [(i, (i + 1) % cores) for i in range(cores)])
+    return lax.ppermute(rows, "sub", [(i, (i + 1) % cores) for i in range(cores)])
+
+
+def per_device(embeddings, labels, doc_block, assign, pattern):
+    chips = lax.axis_size("shard") * lax.axis_size("grp")
+    docs, features = embeddings.shape
+    count = pattern.shape[0]
+    mean = docs // chips
+    slots = -(-(mean + int(3 * math.sqrt(mean))) // 8) * 8
+    rows = chips * slots
+    inputs = (embeddings, labels, doc_block, assign)
     work = cost(2 * rows * rows * features, 2 * rows * features)
+
+    own, slot = send(*inputs, count, 0, slots)
+    other = swap(own)
+    past = own.reshape(chips, slots, features)[:, slots - 1, 2 * LANES : 3 * LANES]
+    past = jnp.max(past.astype(F32), axis=0, keepdims=True)
+    past = jnp.maximum(past, swap(past))[0, 0].astype(jnp.int32)
     best, base, bits = pl.pallas_call(
-        functools.partial(match_own_kernel, chips, segments),
+        functools.partial(match_own_kernel, chips),
         out_shape=(
             jax.ShapeDtypeStruct((rows, LANES), F32),
             jax.ShapeDtypeStruct((rows, LANES), jnp.int32),
@@ -333,64 +374,46 @@
         compiler_params=params(),
         cost_estimate=work,
         name="match_own",
-    )(arrived, pattern)
+    )(own, pattern)
     best = pl.pallas_call(
-        functools.partial(match_other_kernel, chips, segments),
+        functools.partial(match_other_kernel, chips),
         out_shape=jax.ShapeDtypeStruct((chips, LANES), F32),
         in_specs=[in_vmem()] * 5,
         out_specs=in_vmem(),
         compiler_params=params(),
         cost_estimate=work,
         name="match_other",
-    )(arrived, other, best, base, bits)
+    )(own, other, best, base, bits)
+
+    def second_round(size):
+        more, more_slot = send(*inputs, count, slots - 1, size)
+        found = pl.pallas_call(
+            functools.partial(match_more_kernel, chips),
+            out_shape=jax.ShapeDtypeStruct((chips, LANES), F32),
+            in_specs=[in_vmem()] * 6 + [in_smem(), in_vmem()],
+            out_specs=in_vmem(),
+            compiler_params=params(),
+            name="match_more",
+        )(own, other, more, swap(more), base, bits, pattern, best)
+        return found, jnp.where(more_slot >= 0, more_slot + slots, slot), lowest
+
+    def by_general_form():
+        direct = general_form(*inputs, pattern).reshape(1, docs)
+        return best, jnp.full_like(slot, -1), direct
+
+    lowest = jnp.full((1, docs), -1.0, F32)
+    rounds = [lambda: (best, slot, lowest)]
+    rounds += [functools.partial(second_round, size) for size in MORE]
+    best, slot, direct = lax.switch(past, rounds + [by_general_form])
     back = lax.all_to_all(best, ("shard", "grp"), split_axis=0, concat_axis=0, tiled=True)
     return pl.pallas_call(
-        functools.partial(unpack_kernel, chips, slots),
+        functools.partial(unpack_kernel, chips, slots + max(MORE)),
         out_shape=jax.ShapeDtypeStruct((1, docs), F32),
-        in_specs=[in_vmem()] * 2,
+        in_specs=[in_vmem()] * 3,
         out_specs=in_vmem(),
         compiler_params=params(),
         name="unpack",
-    )(back, slot).reshape(docs)
-
-
-def per_device(embeddings, labels, doc_block, assign, pattern):
-    chips = lax.axis_size("shard") * lax.axis_size("grp")
-    docs, features = embeddings.shape
-    count = pattern.shape[0]
-    mean = docs // chips
-    slots = -(-(mean + int(3 * math.sqrt(mean))) // 8) * 8
-    inputs = (embeddings, labels, doc_block, assign)
-
-    arrived, slot = send(*inputs, count, 0, slots)
-    found = match(arrived, slot, pattern, (slots,))
-
-    past = arrived.reshape(chips, slots, features)[:, slots - 1, 2 * LANES : 3 * LANES]
-    past = jnp.max(past.astype(F32), axis=0, keepdims=True)
-    for axis in ("sub", "parts"):
-        size = lax.axis_size(axis)
-        for shift in range(1, size):
-            to = [(i, (i + shift) % size) for i in range(size)]
-            past = jnp.maximum(past, lax.ppermute(past, axis, to))
-
-    def second_round(size):
-        more, more_slot = send(*inputs, count, slots - 1, size)
-        both = jnp.concatenate(
-            [arrived.reshape(chips, slots, features), more.reshape(chips, size, features)], axis=1
-        ).reshape(chips * (slots + size), features)
-        both_slot = jnp.where(more_slot >= 0, more_slot + slots, slot)
-        return match(both, both_slot, pattern, (slots, size))
-
-    def in_rounds(level):
-        if level > len(MORE):
-            return general_form(*inputs, pattern)
-        return lax.cond(
-            past[0, 0] > level,
-            lambda: in_rounds(level + 1),
-            lambda: second_round(MORE[level - 1]) if level else found,
-        )
-
-    return in_rounds(0)
+    )(back, slot, direct).reshape(docs)
 
 
 def solution(mesh):

time: 61 us -> 60.3 us (0.989)
  blocking collectives: 41.6 us -> 51.1 us
  starting transfers between devices: 5.42 us -> 0.57 us
  waiting for transfers between devices: 5.27 us -> 0.5 us
    all_to_all x0 -> x1, blocking collectives: none -> 9.48 us  [per_device(): lax.all_to_all(best, ('shard', 'grp'), split_axis=0, concat_axis=0, tiled...]
    all_to_all x1 -> x0, starting transfers between devices: 3.27 us -> none  [match(): lax.all_to_all(best, ('shard', 'grp'), split_axis=0, concat_axis=0, tiled...]
    all_to_all x1 -> x0, waiting for transfers between devices: 2.72 us -> none  [match(): lax.all_to_all(best, ('shard', 'grp'), split_axis=0, concat_axis=0, tiled...]
    ppermute x3 -> x2, waiting for transfers between devices: 2.55 us -> 0.5 us  [swap(): lax.ppermute(rows, 'sub', [(i, (i + 1) % cores) for i in range(cores)])]
    ppermute x3 -> x2, starting transfers between devices: 2.15 us -> 0.57 us  [swap(): lax.ppermute(rows, 'sub', [(i, (i + 1) % cores) for i in range(cores)])]
  transfers between devices with their start and end apart: 4 -> 2, of which waited for: 3 -> 1; matrix products, arithmetic and copies ran while one was open for 0% -> 0% of each run, Pallas kernels for 7% -> 3%
where the time goes in v4:
time: 60.3 us; the launch traced here: 60.1 us
  blocking collectives  51.1 us (85%)
  Pallas kernels  7.44 us (12%)
    all_to_all x1, blocking collectives, send(): lax.all_to_all(outgoing, ('shard', 'grp'), split_axis=0, concat_axis=0, t...  41.6 us
    all_to_all x1, blocking collectives, per_device(): lax.all_to_all(best, ('shard', 'grp'), split_axis=0, concat_axis=0, tiled...  9.48 us
    pallas_call x1, Pallas kernels, send(): pl.pallas_call(functools.partial(pack_kernel, groups, chips, first, slots...  2.59 us
    pallas_call x1, Pallas kernels, per_device(): pl.pallas_call(functools.partial(match_own_kernel, chips), out_shape=(jax...  2.06 us
    pallas_call x1, Pallas kernels, per_device(): pl.pallas_call(functools.partial(match_other_kernel, chips), out_shape=ja...  1.72 us
  transfers between devices with their start and end apart: 2, of which 1 were waited for; matrix products, arithmetic and copies ran while one was open for 0% of the time, Pallas kernels for 3%

profile of v4, /device:TPU:0, one launch (start us, length us, event | category | flops | bytes accessed | tf_op | source)
XLA Modules:
  0.0 60.1 jit_solution(4278993973138578977)
XLA Ops:
  0.0 0.0 copy-start.4
  0.0 2.6 %pack.5 = (bf16[704,1024]{1,0:T(8,128)(2,1)S(1)}, s32[8,512]{1,0:T(8,128)S(1)}) custom-call(f32[512,1024]{1,0:T(8,128)} %emb_hbm.1, s32[1,512]{1,0:T(1,128)} %bitcast.85, s32[1,512]{1,0:T(1,128)} %bitcast.88, s32[32,128]{1,0:T(8,128)} %bitcast.64), custom_call_target="tpu_custom_call" | custom-call | tf_op jit(solution)/shard_map/pack/pallas_call | solution.py:315
  2.6 41.6 %all_to_all.66 = bf16[8,88,1024]{2,1,0:T(8,128)(2,1)S(1)} all-to-all(bf16[8,88,1024]{2,1,0:T(8,128)(2,1)S(1)} %bitcast.59), channel_id=1, replica_groups=mesh['parts'=2,'shard'=4,'grp'=2,'sub'=2] {'shard','grp'}, dimensions={0} | all-to-all | bytes 2883584 | tf_op jit(solution)/shard_map/all_to_all | solution.py:339
  44.2 0.0 collective-permute-start.9
  44.3 0.6 collective-permute-start.8
  44.8 0.0 copy-done.4
  44.8 2.1 %match_own.1 = (f32[704,128]{1,0:T(8,128)S(1)}, s32[704,128]{1,0:T(8,128)S(1)}, s32[704,128]{1,0:T(8,128)S(1)}) custom-call(bf16[704,1024]{1,0:T(8,128)(2,1)S(1)} %bitcast.68, s32[4,4]{1,0:T(4,128)S(1)} %copy-done.4), custom_call_target="tpu_custom_call" | custom-call | flops 1015021568 | bytes 1441792 | tf_op jit(solution)/shard_map/match_own/pallas_call | solution.py:365
  46.9 0.0 copy-start
  46.9 0.0 copy-start.1
  46.9 0.0 copy-start.2
  46.9 0.0 copy-start.3
  46.9 0.5 collective-permute-done.8
  47.5 0.0 collective-permute-done.9.other_ref
  47.5 1.7 %match_other.1 = f32[8,128]{1,0:T(8,128)S(1)} custom-call(bf16[704,1024]{1,0:T(8,128)(2,1)S(1)} %bitcast.69, bf16[704,1024]{1,0:T(8,128)(2,1)S(1)} %collective-permute-done.9.other_ref, f32[704,128]{1,0:T(8,128)S(1)} %get-tuple-element.108.before_ref, s32[704,128]{1,0:T(8,128)S(1)} %get-tuple-element.109.base_ref, s32[704,128]{1,0:T(8,128)S(1)} %get-tuple-element.110.bits_ref), custom_call_target="tpu_custom_call" | custom-call | flops 1015021568 | bytes 1441792 | tf_op jit(solution)/shard_map/match_other/pallas_call | solution.py:378
  49.2 0.0 copy-done
  49.2 0.0 copy-done.1
  49.2 0.0 copy-done.2
  49.2 0.0 copy-done.3
  49.3 0.3 conditional.1
  49.5 9.5 %all_to_all.67 = f32[8,1,128]{2,1,0:T(1,128)S(1)} all-to-all(f32[8,1,128]{2,1,0:T(1,128)S(1)} %bitcast.77), channel_id=1, replica_groups=mesh['parts'=2,'shard'=4,'grp'=2,'sub'=2] {'shard','grp'}, dimensions={0} | all-to-all | bytes 8192 | tf_op jit(solution)/shard_map/all_to_all | solution.py:408
  59.0 1.1 %unpack.1 = f32[1,512]{1,0:T(1,128)} custom-call(f32[8,128]{1,0:T(8,128)S(1)} %bitcast.62, s32[8,512]{1,0:T(8,128)S(1)} %get-tuple-element.113.slot_ref, f32[1,512]{1,0:T(1,128)S(1)} %get-tuple-element.114.direct_ref), custom_call_target="tpu_custom_call" | custom-call | tf_op jit(solution)/shard_map/unpack/pallas_call | solution.py:409
  (4 shorter events, 0.0 us)
Async XLA Ops:
  0.0 44.8 %copy-start.4 = (s32[4,4]{1,0:T(4,128)S(1)}, s32[4,4]{1,0:T(4,128)}, u32[]{:S(2)}) copy-start(s32[4,4]{1,0:T(4,128)} %pattern_ref.1) | copy-start | bytes 196
  44.2 3.3 %collective-permute-start.9 = (bf16[704,1024]{1,0:T(8,128)(2,1)S(1)}, bf16[704,1024]{1,0:T(8,128)(2,1)S(1)}, u32[]{:S(2)}, u32[]{:S(2)}) collective-permute-start(bf16[704,1024]{1,0:T(8,128)(2,1)S(1)} %bitcast.67), channel_id=1, source_target_pairs={{0,1},{1,0},{2,3},{3,2},{4,5},{5,4},{6,7},{7,6},{8,9},{9,8},{10,11... | collective-permute-start | bytes 4325384 | tf_op jit(solution)/shard_map/ppermute | solution.py:347
  44.3 3.2 %collective-permute-start.8 = (f32[1,128]{1,0:T(1,128)S(1)}, f32[1,128]{1,0:T(1,128)S(1)}, u32[]{:S(2)}, u32[]{:S(2)}) collective-permute-start(f32[1,128]{1,0:T(1,128)S(1)} %bitcast_convert_fusion), channel_id=1, source_target_pairs={{0,1},{1,0},{2,3},{3,2},{4,5},{5,4},{6,7},{7,6},{8,9},{9,8},{10,11... | collective-permute-start | bytes 1544 | tf_op jit(solution)/shard_map/ppermute | solution.py:347
  46.9 2.3 %copy-start = (s32[4096]{0:T(1024)S(1)}, s32[4096]{0:T(1024)}, u32[]{:S(2)}) copy-start(s32[4096]{0:T(1024)} %param.12) | copy-start | bytes 49156
  46.9 2.3 %copy-start.1 = (f32[512,1024]{1,0:T(8,128)S(1)}, f32[512,1024]{1,0:T(8,128)}, u32[]{:S(2)}) copy-start(f32[512,1024]{1,0:T(8,128)} %emb_hbm.1) | copy-start | bytes 6291460
  46.9 2.3 %copy-start.2 = (s32[512]{0:T(512)S(1)}, s32[512]{0:T(512)}, u32[]{:S(2)}) copy-start(s32[512]{0:T(512)} %param.10) | copy-start | bytes 6148
  46.9 2.3 %copy-start.3 = (s32[512]{0:T(512)S(1)}, s32[512]{0:T(512)}, u32[]{:S(2)}) copy-start(s32[512]{0:T(512)} %param.11) | copy-start | bytes 6148

commit v5 on v4

--- a/solution.py
+++ b/solution.py
@@ -12,6 +12,7 @@
 F32 = jnp.float32
 VMEM_LIMIT = 32 * 1024 * 1024
 LANES = 128
+ORDER = [2, 4, 1, 6, 3, 5, 7, 0]
 PIECES = 2
 MORE = (24, 40)
 
@@ -85,14 +86,20 @@
     return returned_max[send_slot]
 
 
+def distances(chips):
+    return ORDER if chips == 8 else list(range(chips - 1, -1, -1))
+
+
 def dot_nt(left, right):
     return lax.dot_general(left, right, (((1,), (1,)), ((), ())), preferred_element_type=F32)
 
 
 def pack_kernel(
-    groups, chips, first, slots, count, emb_hbm, label_hbm, block_hbm, assign_hbm, out_ref,
-    slot_ref, emb_ref, label_ref, block_ref, assign_ref, unit_ref, copied,
+    groups, chips, first, slots, count, me_ref, emb_hbm, label_hbm, block_hbm, assign_hbm, *refs
 ):
+    out_refs, slot_ref = refs[:chips], refs[chips]
+    emb_ref, label_ref, block_ref, assign_ref, unit_ref, copied = refs[chips + 1 :]
+    me = me_ref[0]
     docs, features = emb_hbm.shape
     step = docs // PIECES
     small = [(label_hbm, label_ref), (assign_hbm, assign_ref), (block_hbm, block_ref)]
@@ -128,8 +135,8 @@
         above = ((cluster - start + 1) * chips - 1).astype(F32)
         return jnp.floor((above + 0.5) / extent).astype(jnp.int32)
 
-    home = home_of(labels)
-    beside = jnp.where(labels + 1 < stop, home_of(labels + 1), home)
+    home = home_of(labels) ^ me
+    beside = jnp.where(labels + 1 < stop, home_of(labels + 1) ^ me, home)
 
     chip_id = lax.broadcasted_iota(jnp.int32, (chips, docs), 0)
     member = (chip_id == home) | (chip_id == beside)
@@ -146,7 +153,8 @@
     for more in MORE:
         past = past + jnp.where(most >= slots + more - 2, 1.0, 0.0)
     slot = jnp.where(member & (rank >= 0) & (rank < slots - 1), rank, -1)
-    slot_ref[...] = slot
+    for chip in range(chips):
+        slot_ref[pl.ds(me ^ chip, 1), :] = slot[chip : chip + 1, :]
 
     code = (labels + group + 2) * count + block_ref[...] + 1
     row_id = lax.broadcasted_iota(jnp.int32, (8, docs), 0)
@@ -168,14 +176,21 @@
     step = min(features, 4 * LANES)
     for at in range(0, features, step):
         rows = jnp.dot(picks, unit_ref[:, at : at + step], preferred_element_type=F32)
-        out_ref[:, at : at + step] = rows.astype(BF16)
+        for chip in range(chips):
+            here = rows[chip * slots : (chip + 1) * slots, :]
+            out_refs[chip][:, at : at + step] = here.astype(BF16)
     for chip in range(chips):
         here = slice(chip * slots, (chip + 1) * slots)
         row = [sent[0:1, here], fill, sent[1:2, here], fill, jnp.broadcast_to(past, (1, LANES))]
-        end = (chip + 1) * slots
-        held = out_ref[end - 8 : end, : 3 * LANES].astype(F32)
+        held = out_refs[chip][slots - 8 : slots, : 3 * LANES].astype(F32)
         held = jnp.where(tail, jnp.concatenate(row, axis=1), held)
-        out_ref[end - 8 : end, : 3 * LANES] = held.astype(BF16)
+        out_refs[chip][slots - 8 : slots, : 3 * LANES] = held.astype(BF16)
+
+
+def join_kernel(*refs):
+    slots = refs[0].shape[0]
+    for at, ref in enumerate(refs[:-1]):
+        refs[-1][at * slots : (at + 1) * slots, :] = ref[...]
 
 
 def codes_of(rows_ref, chips):
@@ -246,19 +261,19 @@
 
 
 def match_other_kernel(
-    chips, own_ref, other_ref, before_ref, base_ref, bits_ref, best_ref
+    chips, me_ref, own_ref, other_ref, before_ref, base_ref, bits_ref, best_ref
 ):
     slots = own_ref.shape[0] // chips
     code = codes_of(other_ref, chips)
     best = match_rows(
         own_ref, base_ref[...], bits_ref[...], other_ref, code, False, before_ref[...]
     )
-    for chip, found in enumerate(by_chip(best, chips)):
-        best_ref[chip : chip + 1, 0:slots] = found
+    for chip, found in zip(distances(chips), by_chip(best, chips)):
+        best_ref[pl.ds(me_ref[0] ^ chip, 1), 0:slots] = found
 
 
 def match_more_kernel(
-    chips, own_ref, other_ref, more_ref, more_other_ref, base_ref, bits_ref, pattern_ref,
+    chips, me_ref, own_ref, other_ref, more_ref, more_other_ref, base_ref, bits_ref, pattern_ref,
     before_ref, best_ref,
 ):
     slots, size = own_ref.shape[0] // chips, more_ref.shape[0] // chips
@@ -267,8 +282,8 @@
     base, bits = base_ref[...], bits_ref[...]
     best = match_rows(own_ref, base, bits, more_ref, code, False, best)
     best = match_rows(own_ref, base, bits, more_other_ref, code_other, False, best)
-    for chip, found in enumerate(by_chip(best, chips)):
-        here = slice(chip, chip + 1)
+    for chip, found in zip(distances(chips), by_chip(best, chips)):
+        here = pl.ds(me_ref[0] ^ chip, 1)
         best_ref[here, 0:slots] = jnp.maximum(before_ref[here, 0:slots], found)
 
     base, bits = row_words(code, pattern_ref)
@@ -277,8 +292,8 @@
     best = match_rows(more_ref, base, bits, other_ref, codes_of(other_ref, chips), False, best)
     best = match_rows(more_ref, base, bits, more_ref, code, True, best)
     best = match_rows(more_ref, base, bits, more_other_ref, code_other, False, best)
-    for chip, found in enumerate(by_chip(best, chips)):
-        best_ref[chip : chip + 1, slots : slots + size] = found
+    for chip, found in zip(distances(chips), by_chip(best, chips)):
+        best_ref[pl.ds(me_ref[0] ^ chip, 1), slots : slots + size] = found
 
 
 def unpack_kernel(chips, slots, back_ref, slot_ref, direct_ref, out_ref):
@@ -308,18 +323,16 @@
     return pl.CostEstimate(flops=flops, bytes_accessed=moved, transcendentals=0)
 
 
-def send(embeddings, labels, doc_block, assign, count, first, slots):
+def send(me, embeddings, labels, doc_block, assign, count, first, slots):
     groups = lax.axis_size("shard")
     chips = groups * lax.axis_size("grp")
     docs, features = embeddings.shape
-    outgoing, slot = pl.pallas_call(
+    *outgoing, slot = pl.pallas_call(
         functools.partial(pack_kernel, groups, chips, first, slots, count),
-        out_shape=(
-            jax.ShapeDtypeStruct((chips * slots, features), BF16),
-            jax.ShapeDtypeStruct((chips, docs), jnp.int32),
-        ),
-        in_specs=[pl.BlockSpec(memory_space=pl.ANY)] * 4,
-        out_specs=(in_vmem(), in_vmem()),
+        out_shape=[jax.ShapeDtypeStruct((slots, features), BF16)] * chips
+        + [jax.ShapeDtypeStruct((chips, docs), jnp.int32)],
+        in_specs=[in_smem()] + [pl.BlockSpec(memory_space=pl.ANY)] * 4,
+        out_specs=[in_vmem()] * (chips + 1),
         scratch_shapes=[
             pltpu.VMEM((docs, features), F32),
             pltpu.VMEM((1, docs), jnp.int32),
@@ -331,15 +344,26 @@
         compiler_params=params(),
         name="pack",
     )(
+        me,
         embeddings,
         labels.reshape(1, docs),
         doc_block.reshape(1, docs),
         assign.reshape(-1, LANES),
     )
-    arrived = lax.all_to_all(
-        outgoing, ("shard", "grp"), split_axis=0, concat_axis=0, tiled=True
-    )
-    return arrived, slot
+    arrived = []
+    for away in distances(chips)[:-1]:
+        to = [(chip, chip ^ away) for chip in range(chips)]
+        arrived.append(lax.ppermute(outgoing[away], ("shard", "grp"), to))
+    arrived.append(outgoing[0])
+    joined = pl.pallas_call(
+        join_kernel,
+        out_shape=jax.ShapeDtypeStruct((chips * slots, features), BF16),
+        in_specs=[in_vmem()] * chips,
+        out_specs=in_vmem(),
+        compiler_params=params(),
+        name="join",
+    )(*arrived)
+    return joined, slot
 
 
 def swap(rows):
@@ -354,14 +378,18 @@
     mean = docs // chips
     slots = -(-(mean + int(3 * math.sqrt(mean))) // 8) * 8
     rows = chips * slots
+    me = lax.axis_index(("shard", "grp")).astype(jnp.int32).reshape(1)
     inputs = (embeddings, labels, doc_block, assign)
     work = cost(2 * rows * rows * features, 2 * rows * features)
 
-    own, slot = send(*inputs, count, 0, slots)
+    own, slot = send(me, *inputs, count, 0, slots)
     other = swap(own)
-    past = own.reshape(chips, slots, features)[:, slots - 1, 2 * LANES : 3 * LANES]
-    past = jnp.max(past.astype(F32), axis=0, keepdims=True)
-    past = jnp.maximum(past, swap(past))[0, 0].astype(jnp.int32)
+    ends = [
+        rows_in.reshape(chips, slots, features)[:, slots - 1, 2 * LANES : 3 * LANES]
+        for rows_in in (own, other)
+    ]
+    past = jnp.maximum(*[jnp.max(end.astype(F32), axis=0, keepdims=True) for end in ends])
+    past = past[0, 0].astype(jnp.int32)
     best, base, bits = pl.pallas_call(
         functools.partial(match_own_kernel, chips),
         out_shape=(
@@ -378,23 +406,23 @@
     best = pl.pallas_call(
         functools.partial(match_other_kernel, chips),
         out_shape=jax.ShapeDtypeStruct((chips, LANES), F32),
-        in_specs=[in_vmem()] * 5,
+        in_specs=[in_smem()] + [in_vmem()] * 5,
         out_specs=in_vmem(),
         compiler_params=params(),
         cost_estimate=work,
         name="match_other",
-    )(own, other, best, base, bits)
+    )(me, own, other, best, base, bits)
 
     def second_round(size):
-        more, more_slot = send(*inputs, count, slots - 1, size)
+        more, more_slot = send(me, *inputs, count, slots - 1, size)
         found = pl.pallas_call(
             functools.partial(match_more_kernel, chips),
             out_shape=jax.ShapeDtypeStruct((chips, LANES), F32),
-            in_specs=[in_vmem()] * 6 + [in_smem(), in_vmem()],
+            in_specs=[in_smem()] + [in_vmem()] * 6 + [in_smem(), in_vmem()],
             out_specs=in_vmem(),
             compiler_params=params(),
             name="match_more",
-        )(own, other, more, swap(more), base, bits, pattern, best)
+        )(me, own, other, more, swap(more), base, bits, pattern, best)
         return found, jnp.where(more_slot >= 0, more_slot + slots, slot), lowest
 
     def by_general_form():

time: 60.3 us -> 56.5 us (0.937)
  blocking collectives: 51.1 us -> 11.5 us
  waiting for transfers between devices: 0.5 us -> 22.1 us
  starting transfers between devices: 0.57 us -> 14.7 us
    all_to_all x1 -> x0, blocking collectives: 41.6 us -> none  [send(): lax.all_to_all(outgoing, ('shard', 'grp'), split_axis=0, concat_axis=0, t...]
    ppermute x0 -> x7, waiting for transfers between devices: none -> 21 us  [send(): arrived.append(lax.ppermute(outgoing[away], ('shard', 'grp'), to))]
    ppermute x0 -> x7, starting transfers between devices: none -> 14.6 us  [send(): arrived.append(lax.ppermute(outgoing[away], ('shard', 'grp'), to))]
    all_to_all x1, blocking collectives: 9.48 us -> 11.5 us  [per_device(): lax.all_to_all(best, ('shard', 'grp'), split_axis=0, concat_axis=0, tiled...]
  transfers between devices with their start and end apart: 2 -> 8, of which waited for: 1 -> 4; matrix products, arithmetic and copies ran while one was open for 0% -> 0% of each run, Pallas kernels for 3% -> 4%
where the time goes in v5:
time: 56.5 us; the launch traced here: 56.3 us
  waiting for transfers between devices  22.1 us (39%)
  starting transfers between devices  14.7 us (26%)
  blocking collectives  11.5 us (20%)
  Pallas kernels  7.5 us (13%)
    ppermute x7, waiting for transfers between devices, send(): arrived.append(lax.ppermute(outgoing[away], ('shard', 'grp'), to))  21 us
    ppermute x7, starting transfers between devices, send(): arrived.append(lax.ppermute(outgoing[away], ('shard', 'grp'), to))  14.6 us
    all_to_all x1, blocking collectives, per_device(): lax.all_to_all(best, ('shard', 'grp'), split_axis=0, concat_axis=0, tiled...  11.5 us
    pallas_call x1, Pallas kernels, send(): pl.pallas_call(functools.partial(pack_kernel, groups, chips, first, slots...  2.59 us
    pallas_call x1, Pallas kernels, per_device(): pl.pallas_call(functools.partial(match_own_kernel, chips), out_shape=(jax...  2.05 us
    pallas_call x1, Pallas kernels, per_device(): pl.pallas_call(functools.partial(match_other_kernel, chips), out_shape=ja...  1.71 us
  transfers between devices with their start and end apart: 8, of which 4 were waited for; matrix products, arithmetic and copies ran while one was open for 0% of the time, Pallas kernels for 4%

profile of v5, /device:TPU:0, one launch (start us, length us, event | category | flops | bytes accessed | tf_op | source)
XLA Modules:
  0.0 56.3 jit_solution(7323255767112796215)
XLA Ops:
  0.0 0.0 copy-start.4
  0.0 2.6 %pack.5 = (bf16[88,1024]{1,0:T(8,128)(2,1)S(1)}, bf16[88,1024]{1,0:T(8,128)(2,1)S(1)}, bf16[88,1024]{1,0:T(8,128)(2,1)S(1)}, bf16[88,1024]{1,0:T(8,128)(2,1)S(1)...) custom-call(s32[1]{0:T(128)} %bitcast.17.me_ref, ...), custom_call_target="tpu_custom_call" | custom-call | tf_op jit(solution)/shard_map/pack/pallas_call | solution.py:330
  2.6 3.1 %collective-permute-start.22 = (bf16[88,1024]{1,0:T(8,128)(2,1)S(1)}, bf16[88,1024]{1,0:T(8,128)(2,1)S(1)}, u32[]{:S(2)}, u32[]{:S(2)}) collective-permute-start(bf16[88,1024]{1,0:T(8,128)(2,1)S(1)} %get-tuple-element.134), channel_id=1, source_target_pairs={{0,4},{2,6},{4,0},{6,2},{8,12},{10,14},{12,8},{14,10},{1,5},{3,7},... | collective-permute-start | bytes 540680 | tf_op jit(solution)/shard_map/ppermute | solution.py:356
  5.7 2.6 %collective-permute-start.23 = (bf16[88,1024]{1,0:T(8,128)(2,1)S(1)}, bf16[88,1024]{1,0:T(8,128)(2,1)S(1)}, u32[]{:S(2)}, u32[]{:S(2)}) collective-permute-start(bf16[88,1024]{1,0:T(8,128)(2,1)S(1)} %get-tuple-element.135), channel_id=1, source_target_pairs={{0,8},{2,10},{4,12},{6,14},{8,0},{10,2},{12,4},{14,6},{1,9},{3,11}... | collective-permute-start | bytes 540680 | tf_op jit(solution)/shard_map/ppermute | solution.py:356
  8.3 1.5 %collective-permute-start.24 = (bf16[88,1024]{1,0:T(8,128)(2,1)S(1)}, bf16[88,1024]{1,0:T(8,128)(2,1)S(1)}, u32[]{:S(2)}, u32[]{:S(2)}) collective-permute-start(bf16[88,1024]{1,0:T(8,128)(2,1)S(1)} %get-tuple-element.136), channel_id=1, source_target_pairs={{0,2},{2,0},{4,6},{6,4},{8,10},{10,8},{12,14},{14,12},{1,3},{3,1},... | collective-permute-start | bytes 540680 | tf_op jit(solution)/shard_map/ppermute | solution.py:356
  9.8 0.2 collective-permute-start.25
  10.0 0.6 %collective-permute-start.26 = (bf16[88,1024]{1,0:T(8,128)(2,1)S(1)}, bf16[88,1024]{1,0:T(8,128)(2,1)S(1)}, u32[]{:S(2)}, u32[]{:S(2)}) collective-permute-start(bf16[88,1024]{1,0:T(8,128)(2,1)S(1)} %get-tuple-element.138), channel_id=1, source_target_pairs={{0,6},{2,4},{4,2},{6,0},{8,14},{10,12},{12,10},{14,8},{1,7},{3,5},... | collective-permute-start | bytes 540680 | tf_op jit(solution)/shard_map/ppermute | solution.py:356
  10.6 3.5 %collective-permute-done.22.refs_0_ = bf16[88,1024]{1,0:T(8,128)(2,1)S(1)} collective-permute-done((bf16[88,1024]{1,0:T(8,128)(2,1)S(1)}, bf16[88,1024]{1,0:T(8,128)(2,1)S(1)}, u32[]{:S(2)}, u32[]{:S(2)}) %collective-permute-start.22) | collective-permute-done | bytes 180256 | tf_op jit(solution)/shard_map/ppermute | solution.py:356
  14.2 3.1 %collective-permute-start.27 = (bf16[88,1024]{1,0:T(8,128)(2,1)S(1)}, bf16[88,1024]{1,0:T(8,128)(2,1)S(1)}, u32[]{:S(2)}, u32[]{:S(2)}) collective-permute-start(bf16[88,1024]{1,0:T(8,128)(2,1)S(1)} %get-tuple-element.139), channel_id=1, source_target_pairs={{0,10},{2,8},{4,14},{6,12},{8,2},{10,0},{12,6},{14,4},{1,11},{3,9}... | collective-permute-start | bytes 540680 | tf_op jit(solution)/shard_map/ppermute | solution.py:356
  17.3 4.5 %collective-permute-done.23.refs_1_ = bf16[88,1024]{1,0:T(8,128)(2,1)S(1)} collective-permute-done((bf16[88,1024]{1,0:T(8,128)(2,1)S(1)}, bf16[88,1024]{1,0:T(8,128)(2,1)S(1)}, u32[]{:S(2)}, u32[]{:S(2)}) %collective-permute-start.23) | collective-permute-done | bytes 180256 | tf_op jit(solution)/shard_map/ppermute | solution.py:356
  21.8 3.5 %collective-permute-start.28 = (bf16[88,1024]{1,0:T(8,128)(2,1)S(1)}, bf16[88,1024]{1,0:T(8,128)(2,1)S(1)}, u32[]{:S(2)}, u32[]{:S(2)}) collective-permute-start(bf16[88,1024]{1,0:T(8,128)(2,1)S(1)} %get-tuple-element.140), channel_id=1, source_target_pairs={{0,14},{2,12},{4,10},{6,8},{8,6},{10,4},{12,2},{14,0},{1,15},{3,13... | collective-permute-start | bytes 540680 | tf_op jit(solution)/shard_map/ppermute | solution.py:356
  25.3 0.0 collective-permute-done.24.refs_2_
  25.3 0.0 collective-permute-done.25.refs_3_
  25.3 0.0 collective-permute-done.26.refs_4_
  25.3 12.9 %collective-permute-done.27.refs_5_ = bf16[88,1024]{1,0:T(8,128)(2,1)S(1)} collective-permute-done((bf16[88,1024]{1,0:T(8,128)(2,1)S(1)}, bf16[88,1024]{1,0:T(8,128)(2,1)S(1)}, u32[]{:S(2)}, u32[]{:S(2)}) %collective-permute-start.27) | collective-permute-done | bytes 180256 | tf_op jit(solution)/shard_map/ppermute | solution.py:356
  38.2 0.0 collective-permute-done.28.refs_6_
  38.2 0.1 join.5.own_ref
  38.3 0.1 collective-permute-start.29
  38.4 0.0 copy-done.4
  38.4 2.0 %match_own.1 = (f32[704,128]{1,0:T(8,128)S(1)}, s32[704,128]{1,0:T(8,128)S(1)}, s32[704,128]{1,0:T(8,128)S(1)}) custom-call(bf16[704,1024]{1,0:T(8,128)(2,1)S(1)} %join.5.own_ref, s32[4,4]{1,0:T(4,128)S(1)} %copy-done.4), custom_call_target="tpu_custom_call" | custom-call | flops 1015021568 | bytes 1441792 | tf_op jit(solution)/shard_map/match_own/pallas_call | solution.py:393
  40.5 0.0 copy-start
  40.5 0.0 copy-start.1
  40.5 0.0 copy-start.2
  40.5 0.0 copy-start.3
  40.5 1.1 %collective-permute-done.29.other_ref = bf16[704,1024]{1,0:T(8,128)(2,1)S(1)} collective-permute-done((bf16[704,1024]{1,0:T(8,128)(2,1)S(1)}, bf16[704,1024]{1,0:T(8,128)(2,1)S(1)}, u32[]{:S(2)}, u32[]{:S(2)}) %collective-permute-start.29) | collective-permute-done | bytes 1441824 | tf_op jit(solution)/shard_map/ppermute | solution.py:371
  41.6 1.7 %match_other.1 = f32[8,128]{1,0:T(8,128)S(1)} custom-call(s32[1]{0:T(128)} %bitcast.17.me_ref, bf16[704,1024]{1,0:T(8,128)(2,1)S(1)} %join.5.own_ref, bf16[704,1024]{1,0:T(8,128)(2,1)S(1)} %collective-permute-done.29.other_ref, f32[704,128]{1,0:T(8,128)S(1)} %get-tuple-element.142.before_ref, s32[704,128]{1,0:T(8,128)S(1)} %get-tuple-element.143.base_ref, ...), custom_call_target="tpu_custom_call" | custom-call | flops 1015021568 | bytes 1441792 | tf_op jit(solution)/shard_map/match_other/pallas_call | solution.py:406
  43.4 0.0 copy-done
  43.4 0.0 copy-done.1
  43.4 0.0 copy-done.2
  43.4 0.0 copy-done.3
  43.4 0.3 conditional.1
  43.7 11.5 %all_to_all.37 = f32[8,1,128]{2,1,0:T(1,128)S(1)} all-to-all(f32[8,1,128]{2,1,0:T(1,128)S(1)} %bitcast.61), channel_id=1, replica_groups=mesh['parts'=2,'shard'=4,'grp'=2,'sub'=2] {'shard','grp'}, dimensions={0} | all-to-all | bytes 8192 | tf_op jit(solution)/shard_map/all_to_all | solution.py:436
  55.2 1.1 %unpack.1 = f32[1,512]{1,0:T(1,128)} custom-call(f32[8,128]{1,0:T(8,128)S(1)} %bitcast.49, s32[8,512]{1,0:T(8,128)S(1)} %get-tuple-element.147.slot_ref, f32[1,512]{1,0:T(1,128)S(1)} %get-tuple-element.148.direct_ref), custom_call_target="tpu_custom_call" | custom-call | tf_op jit(solution)/shard_map/unpack/pallas_call | solution.py:437
  (4 shorter events, 0.1 us)
Async XLA Ops:
  0.0 38.4 %copy-start.4 = (s32[4,4]{1,0:T(4,128)S(1)}, s32[4,4]{1,0:T(4,128)}, u32[]{:S(2)}) copy-start(s32[4,4]{1,0:T(4,128)} %pattern_ref.1) | copy-start | bytes 196
  2.6 11.6 %collective-permute-start.22 = (bf16[88,1024]{1,0:T(8,128)(2,1)S(1)}, bf16[88,1024]{1,0:T(8,128)(2,1)S(1)}, u32[]{:S(2)}, u32[]{:S(2)}) collective-permute-start(bf16[88,1024]{1,0:T(8,128)(2,1)S(1)} %get-tuple-element.134), channel_id=1, source_target_pairs={{0,4},{2,6},{4,0},{6,2},{8,12},{10,14},{12,8},{14,10},{1,5},{3,7},... | collective-permute-start | bytes 540680 | tf_op jit(solution)/shard_map/ppermute | solution.py:356
  5.7 16.1 %collective-permute-start.23 = (bf16[88,1024]{1,0:T(8,128)(2,1)S(1)}, bf16[88,1024]{1,0:T(8,128)(2,1)S(1)}, u32[]{:S(2)}, u32[]{:S(2)}) collective-permute-start(bf16[88,1024]{1,0:T(8,128)(2,1)S(1)} %get-tuple-element.135), channel_id=1, source_target_pairs={{0,8},{2,10},{4,12},{6,14},{8,0},{10,2},{12,4},{14,6},{1,9},{3,11}... | collective-permute-start | bytes 540680 | tf_op jit(solution)/shard_map/ppermute | solution.py:356
  8.3 17.0 %collective-permute-start.24 = (bf16[88,1024]{1,0:T(8,128)(2,1)S(1)}, bf16[88,1024]{1,0:T(8,128)(2,1)S(1)}, u32[]{:S(2)}, u32[]{:S(2)}) collective-permute-start(bf16[88,1024]{1,0:T(8,128)(2,1)S(1)} %get-tuple-element.136), channel_id=1, source_target_pairs={{0,2},{2,0},{4,6},{6,4},{8,10},{10,8},{12,14},{14,12},{1,3},{3,1},... | collective-permute-start | bytes 540680 | tf_op jit(solution)/shard_map/ppermute | solution.py:356
  9.8 15.5 %collective-permute-start.25 = (bf16[88,1024]{1,0:T(8,128)(2,1)S(1)}, bf16[88,1024]{1,0:T(8,128)(2,1)S(1)}, u32[]{:S(2)}, u32[]{:S(2)}) collective-permute-start(bf16[88,1024]{1,0:T(8,128)(2,1)S(1)} %get-tuple-element.137), channel_id=1, source_target_pairs={{0,12},{2,14},{4,8},{6,10},{8,4},{10,6},{12,0},{14,2},{1,13},{3,15... | collective-permute-start | bytes 540680 | tf_op jit(solution)/shard_map/ppermute | solution.py:356
  10.0 15.3 %collective-permute-start.26 = (bf16[88,1024]{1,0:T(8,128)(2,1)S(1)}, bf16[88,1024]{1,0:T(8,128)(2,1)S(1)}, u32[]{:S(2)}, u32[]{:S(2)}) collective-permute-start(bf16[88,1024]{1,0:T(8,128)(2,1)S(1)} %get-tuple-element.138), channel_id=1, source_target_pairs={{0,6},{2,4},{4,2},{6,0},{8,14},{10,12},{12,10},{14,8},{1,7},{3,5},... | collective-permute-start | bytes 540680 | tf_op jit(solution)/shard_map/ppermute | solution.py:356
  14.2 24.0 %collective-permute-start.27 = (bf16[88,1024]{1,0:T(8,128)(2,1)S(1)}, bf16[88,1024]{1,0:T(8,128)(2,1)S(1)}, u32[]{:S(2)}, u32[]{:S(2)}) collective-permute-start(bf16[88,1024]{1,0:T(8,128)(2,1)S(1)} %get-tuple-element.139), channel_id=1, source_target_pairs={{0,10},{2,8},{4,14},{6,12},{8,2},{10,0},{12,6},{14,4},{1,11},{3,9}... | collective-permute-start | bytes 540680 | tf_op jit(solution)/shard_map/ppermute | solution.py:356
  21.8 16.4 %collective-permute-start.28 = (bf16[88,1024]{1,0:T(8,128)(2,1)S(1)}, bf16[88,1024]{1,0:T(8,128)(2,1)S(1)}, u32[]{:S(2)}, u32[]{:S(2)}) collective-permute-start(bf16[88,1024]{1,0:T(8,128)(2,1)S(1)} %get-tuple-element.140), channel_id=1, source_target_pairs={{0,14},{2,12},{4,10},{6,8},{8,6},{10,4},{12,2},{14,0},{1,15},{3,13... | collective-permute-start | bytes 540680 | tf_op jit(solution)/shard_map/ppermute | solution.py:356
  38.3 3.3 %collective-permute-start.29 = (bf16[704,1024]{1,0:T(8,128)(2,1)S(1)}, bf16[704,1024]{1,0:T(8,128)(2,1)S(1)}, u32[]{:S(2)}, u32[]{:S(2)}) collective-permute-start(bf16[704,1024]{1,0:T(8,128)(2,1)S(1)} %join.5.own_ref), channel_id=1, source_target_pairs={{0,1},{1,0},{2,3},{3,2},{4,5},{5,4},{6,7},{7,6},{8,9},{9,8},{10,11... | collective-permute-start | bytes 4325384 | tf_op jit(solution)/shard_map/ppermute | solution.py:371
  40.5 2.9 %copy-start = (s32[4096]{0:T(1024)S(1)}, s32[4096]{0:T(1024)}, u32[]{:S(2)}) copy-start(s32[4096]{0:T(1024)} %param.12) | copy-start | bytes 49156
  40.5 2.9 %copy-start.1 = (f32[512,1024]{1,0:T(8,128)S(1)}, f32[512,1024]{1,0:T(8,128)}, u32[]{:S(2)}) copy-start(f32[512,1024]{1,0:T(8,128)} %emb_hbm.1) | copy-start | bytes 6291460
  40.5 2.9 %copy-start.2 = (s32[512]{0:T(512)S(1)}, s32[512]{0:T(512)}, u32[]{:S(2)}) copy-start(s32[512]{0:T(512)} %param.10) | copy-start | bytes 6148
  40.5 2.9 %copy-start.3 = (s32[512]{0:T(512)S(1)}, s32[512]{0:T(512)}, u32[]{:S(2)}) copy-start(s32[512]{0:T(512)} %param.11) | copy-start | bytes 6148

commit v6 on v5

--- a/solution.py
+++ b/solution.py
@@ -14,7 +14,7 @@
 LANES = 128
 ORDER = [2, 4, 1, 6, 3, 5, 7, 0]
 PIECES = 2
-MORE = (24, 40)
+MORE = (8, 24, 40)
 
 
 def row_masks(doc_codes, pattern):

time: 56.5 us -> 56.5 us (level)
  no operation moved by 1% of the time
where the time goes in v6:
time: 56.5 us; the launch traced here: 56.3 us
  waiting for transfers between devices  22 us (39%)
  starting transfers between devices  14.7 us (26%)
  blocking collectives  11.6 us (21%)
  Pallas kernels  7.53 us (13%)
    ppermute x7, waiting for transfers between devices, send(): arrived.append(lax.ppermute(outgoing[away], ('shard', 'grp'), to))  21 us
    ppermute x7, starting transfers between devices, send(): arrived.append(lax.ppermute(outgoing[away], ('shard', 'grp'), to))  14.6 us
    all_to_all x1, blocking collectives, per_device(): lax.all_to_all(best, ('shard', 'grp'), split_axis=0, concat_axis=0, tiled...  11.6 us
    pallas_call x1, Pallas kernels, send(): pl.pallas_call(functools.partial(pack_kernel, groups, chips, first, slots...  2.59 us
    pallas_call x1, Pallas kernels, per_device(): pl.pallas_call(functools.partial(match_own_kernel, chips), out_shape=(jax...  2.07 us
    pallas_call x1, Pallas kernels, per_device(): pl.pallas_call(functools.partial(match_other_kernel, chips), out_shape=ja...  1.72 us
  transfers between devices with their start and end apart: 8, of which 4 were waited for; matrix products, arithmetic and copies ran while one was open for 0% of the time, Pallas kernels for 4%

profile of v6, /device:TPU:0, one launch (start us, length us, event | category | flops | bytes accessed | tf_op | source)
XLA Modules:
  0.0 56.3 jit_solution(1564365177870094202)
XLA Ops:
  0.0 0.0 copy-start.4
  0.0 2.6 %pack.7 = (bf16[88,1024]{1,0:T(8,128)(2,1)S(1)}, bf16[88,1024]{1,0:T(8,128)(2,1)S(1)}, bf16[88,1024]{1,0:T(8,128)(2,1)S(1)}, bf16[88,1024]{1,0:T(8,128)(2,1)S(1)...) custom-call(s32[1]{0:T(128)} %bitcast.20.me_ref, ...), custom_call_target="tpu_custom_call" | custom-call | tf_op jit(solution)/shard_map/pack/pallas_call | solution.py:330
  2.6 3.1 %collective-permute-start.30 = (bf16[88,1024]{1,0:T(8,128)(2,1)S(1)}, bf16[88,1024]{1,0:T(8,128)(2,1)S(1)}, u32[]{:S(2)}, u32[]{:S(2)}) collective-permute-start(bf16[88,1024]{1,0:T(8,128)(2,1)S(1)} %get-tuple-element.179), channel_id=1, source_target_pairs={{0,4},{2,6},{4,0},{6,2},{8,12},{10,14},{12,8},{14,10},{1,5},{3,7},... | collective-permute-start | bytes 540680 | tf_op jit(solution)/shard_map/ppermute | solution.py:356
  5.7 2.6 %collective-permute-start.31 = (bf16[88,1024]{1,0:T(8,128)(2,1)S(1)}, bf16[88,1024]{1,0:T(8,128)(2,1)S(1)}, u32[]{:S(2)}, u32[]{:S(2)}) collective-permute-start(bf16[88,1024]{1,0:T(8,128)(2,1)S(1)} %get-tuple-element.180), channel_id=1, source_target_pairs={{0,8},{2,10},{4,12},{6,14},{8,0},{10,2},{12,4},{14,6},{1,9},{3,11}... | collective-permute-start | bytes 540680 | tf_op jit(solution)/shard_map/ppermute | solution.py:356
  8.3 1.5 %collective-permute-start.32 = (bf16[88,1024]{1,0:T(8,128)(2,1)S(1)}, bf16[88,1024]{1,0:T(8,128)(2,1)S(1)}, u32[]{:S(2)}, u32[]{:S(2)}) collective-permute-start(bf16[88,1024]{1,0:T(8,128)(2,1)S(1)} %get-tuple-element.181), channel_id=1, source_target_pairs={{0,2},{2,0},{4,6},{6,4},{8,10},{10,8},{12,14},{14,12},{1,3},{3,1},... | collective-permute-start | bytes 540680 | tf_op jit(solution)/shard_map/ppermute | solution.py:356
  9.8 0.2 collective-permute-start.33
  10.0 0.6 %collective-permute-start.34 = (bf16[88,1024]{1,0:T(8,128)(2,1)S(1)}, bf16[88,1024]{1,0:T(8,128)(2,1)S(1)}, u32[]{:S(2)}, u32[]{:S(2)}) collective-permute-start(bf16[88,1024]{1,0:T(8,128)(2,1)S(1)} %get-tuple-element.183), channel_id=1, source_target_pairs={{0,6},{2,4},{4,2},{6,0},{8,14},{10,12},{12,10},{14,8},{1,7},{3,5},... | collective-permute-start | bytes 540680 | tf_op jit(solution)/shard_map/ppermute | solution.py:356
  10.6 3.5 %collective-permute-done.30.refs_0_ = bf16[88,1024]{1,0:T(8,128)(2,1)S(1)} collective-permute-done((bf16[88,1024]{1,0:T(8,128)(2,1)S(1)}, bf16[88,1024]{1,0:T(8,128)(2,1)S(1)}, u32[]{:S(2)}, u32[]{:S(2)}) %collective-permute-start.30) | collective-permute-done | bytes 180256 | tf_op jit(solution)/shard_map/ppermute | solution.py:356
  14.2 3.1 %collective-permute-start.35 = (bf16[88,1024]{1,0:T(8,128)(2,1)S(1)}, bf16[88,1024]{1,0:T(8,128)(2,1)S(1)}, u32[]{:S(2)}, u32[]{:S(2)}) collective-permute-start(bf16[88,1024]{1,0:T(8,128)(2,1)S(1)} %get-tuple-element.184), channel_id=1, source_target_pairs={{0,10},{2,8},{4,14},{6,12},{8,2},{10,0},{12,6},{14,4},{1,11},{3,9}... | collective-permute-start | bytes 540680 | tf_op jit(solution)/shard_map/ppermute | solution.py:356
  17.3 4.5 %collective-permute-done.31.refs_1_ = bf16[88,1024]{1,0:T(8,128)(2,1)S(1)} collective-permute-done((bf16[88,1024]{1,0:T(8,128)(2,1)S(1)}, bf16[88,1024]{1,0:T(8,128)(2,1)S(1)}, u32[]{:S(2)}, u32[]{:S(2)}) %collective-permute-start.31) | collective-permute-done | bytes 180256 | tf_op jit(solution)/shard_map/ppermute | solution.py:356
  21.8 3.5 %collective-permute-start.36 = (bf16[88,1024]{1,0:T(8,128)(2,1)S(1)}, bf16[88,1024]{1,0:T(8,128)(2,1)S(1)}, u32[]{:S(2)}, u32[]{:S(2)}) collective-permute-start(bf16[88,1024]{1,0:T(8,128)(2,1)S(1)} %get-tuple-element.185), channel_id=1, source_target_pairs={{0,14},{2,12},{4,10},{6,8},{8,6},{10,4},{12,2},{14,0},{1,15},{3,13... | collective-permute-start | bytes 540680 | tf_op jit(solution)/shard_map/ppermute | solution.py:356
  25.3 0.0 collective-permute-done.32.refs_2_
  25.3 0.0 collective-permute-done.33.refs_3_
  25.3 0.0 collective-permute-done.34.refs_4_
  25.3 12.9 %collective-permute-done.35.refs_5_ = bf16[88,1024]{1,0:T(8,128)(2,1)S(1)} collective-permute-done((bf16[88,1024]{1,0:T(8,128)(2,1)S(1)}, bf16[88,1024]{1,0:T(8,128)(2,1)S(1)}, u32[]{:S(2)}, u32[]{:S(2)}) %collective-permute-start.35) | collective-permute-done | bytes 180256 | tf_op jit(solution)/shard_map/ppermute | solution.py:356
  38.2 0.0 collective-permute-done.36.refs_6_
  38.2 0.1 join.7.own_ref
  38.3 0.1 collective-permute-start.37
  38.4 0.0 copy-done.4
  38.4 2.1 %match_own.1 = (f32[704,128]{1,0:T(8,128)S(1)}, s32[704,128]{1,0:T(8,128)S(1)}, s32[704,128]{1,0:T(8,128)S(1)}) custom-call(bf16[704,1024]{1,0:T(8,128)(2,1)S(1)} %join.7.own_ref, s32[4,4]{1,0:T(4,128)S(1)} %copy-done.4), custom_call_target="tpu_custom_call" | custom-call | flops 1015021568 | bytes 1441792 | tf_op jit(solution)/shard_map/match_own/pallas_call | solution.py:393
  40.5 0.0 copy-start
  40.5 0.0 copy-start.1
  40.5 0.0 copy-start.2
  40.5 0.0 copy-start.3
  40.5 1.0 %collective-permute-done.37.other_ref = bf16[704,1024]{1,0:T(8,128)(2,1)S(1)} collective-permute-done((bf16[704,1024]{1,0:T(8,128)(2,1)S(1)}, bf16[704,1024]{1,0:T(8,128)(2,1)S(1)}, u32[]{:S(2)}, u32[]{:S(2)}) %collective-permute-start.37) | collective-permute-done | bytes 1441824 | tf_op jit(solution)/shard_map/ppermute | solution.py:371
  41.6 1.7 %match_other.1 = f32[8,128]{1,0:T(8,128)S(1)} custom-call(s32[1]{0:T(128)} %bitcast.20.me_ref, bf16[704,1024]{1,0:T(8,128)(2,1)S(1)} %join.7.own_ref, bf16[704,1024]{1,0:T(8,128)(2,1)S(1)} %collective-permute-done.37.other_ref, f32[704,128]{1,0:T(8,128)S(1)} %get-tuple-element.187.before_ref, s32[704,128]{1,0:T(8,128)S(1)} %get-tuple-element.188.base_ref, ...), custom_call_target="tpu_custom_call" | custom-call | flops 1015021568 | bytes 1441792 | tf_op jit(solution)/shard_map/match_other/pallas_call | solution.py:406
  43.4 0.0 copy-done
  43.4 0.0 copy-done.1
  43.4 0.0 copy-done.2
  43.4 0.0 copy-done.3
  43.4 0.3 conditional.1
  43.7 11.6 %all_to_all.37 = f32[8,1,128]{2,1,0:T(1,128)S(1)} all-to-all(f32[8,1,128]{2,1,0:T(1,128)S(1)} %bitcast.65), channel_id=1, replica_groups=mesh['parts'=2,'shard'=4,'grp'=2,'sub'=2] {'shard','grp'}, dimensions={0} | all-to-all | bytes 8192 | tf_op jit(solution)/shard_map/all_to_all | solution.py:436
  55.3 1.1 %unpack.1 = f32[1,512]{1,0:T(1,128)} custom-call(f32[8,128]{1,0:T(8,128)S(1)} %bitcast.52, s32[8,512]{1,0:T(8,128)S(1)} %get-tuple-element.192.slot_ref, f32[1,512]{1,0:T(1,128)S(1)} %get-tuple-element.193.direct_ref), custom_call_target="tpu_custom_call" | custom-call | tf_op jit(solution)/shard_map/unpack/pallas_call | solution.py:437
  (4 shorter events, 0.1 us)
Async XLA Ops:
  0.0 38.4 %copy-start.4 = (s32[4,4]{1,0:T(4,128)S(1)}, s32[4,4]{1,0:T(4,128)}, u32[]{:S(2)}) copy-start(s32[4,4]{1,0:T(4,128)} %pattern_ref.1) | copy-start | bytes 196
  2.6 11.6 %collective-permute-start.30 = (bf16[88,1024]{1,0:T(8,128)(2,1)S(1)}, bf16[88,1024]{1,0:T(8,128)(2,1)S(1)}, u32[]{:S(2)}, u32[]{:S(2)}) collective-permute-start(bf16[88,1024]{1,0:T(8,128)(2,1)S(1)} %get-tuple-element.179), channel_id=1, source_target_pairs={{0,4},{2,6},{4,0},{6,2},{8,12},{10,14},{12,8},{14,10},{1,5},{3,7},... | collective-permute-start | bytes 540680 | tf_op jit(solution)/shard_map/ppermute | solution.py:356
  5.7 16.1 %collective-permute-start.31 = (bf16[88,1024]{1,0:T(8,128)(2,1)S(1)}, bf16[88,1024]{1,0:T(8,128)(2,1)S(1)}, u32[]{:S(2)}, u32[]{:S(2)}) collective-permute-start(bf16[88,1024]{1,0:T(8,128)(2,1)S(1)} %get-tuple-element.180), channel_id=1, source_target_pairs={{0,8},{2,10},{4,12},{6,14},{8,0},{10,2},{12,4},{14,6},{1,9},{3,11}... | collective-permute-start | bytes 540680 | tf_op jit(solution)/shard_map/ppermute | solution.py:356
  8.3 17.0 %collective-permute-start.32 = (bf16[88,1024]{1,0:T(8,128)(2,1)S(1)}, bf16[88,1024]{1,0:T(8,128)(2,1)S(1)}, u32[]{:S(2)}, u32[]{:S(2)}) collective-permute-start(bf16[88,1024]{1,0:T(8,128)(2,1)S(1)} %get-tuple-element.181), channel_id=1, source_target_pairs={{0,2},{2,0},{4,6},{6,4},{8,10},{10,8},{12,14},{14,12},{1,3},{3,1},... | collective-permute-start | bytes 540680 | tf_op jit(solution)/shard_map/ppermute | solution.py:356
  9.8 15.5 %collective-permute-start.33 = (bf16[88,1024]{1,0:T(8,128)(2,1)S(1)}, bf16[88,1024]{1,0:T(8,128)(2,1)S(1)}, u32[]{:S(2)}, u32[]{:S(2)}) collective-permute-start(bf16[88,1024]{1,0:T(8,128)(2,1)S(1)} %get-tuple-element.182), channel_id=1, source_target_pairs={{0,12},{2,14},{4,8},{6,10},{8,4},{10,6},{12,0},{14,2},{1,13},{3,15... | collective-permute-start | bytes 540680 | tf_op jit(solution)/shard_map/ppermute | solution.py:356
  10.0 15.3 %collective-permute-start.34 = (bf16[88,1024]{1,0:T(8,128)(2,1)S(1)}, bf16[88,1024]{1,0:T(8,128)(2,1)S(1)}, u32[]{:S(2)}, u32[]{:S(2)}) collective-permute-start(bf16[88,1024]{1,0:T(8,128)(2,1)S(1)} %get-tuple-element.183), channel_id=1, source_target_pairs={{0,6},{2,4},{4,2},{6,0},{8,14},{10,12},{12,10},{14,8},{1,7},{3,5},... | collective-permute-start | bytes 540680 | tf_op jit(solution)/shard_map/ppermute | solution.py:356
  14.2 24.0 %collective-permute-start.35 = (bf16[88,1024]{1,0:T(8,128)(2,1)S(1)}, bf16[88,1024]{1,0:T(8,128)(2,1)S(1)}, u32[]{:S(2)}, u32[]{:S(2)}) collective-permute-start(bf16[88,1024]{1,0:T(8,128)(2,1)S(1)} %get-tuple-element.184), channel_id=1, source_target_pairs={{0,10},{2,8},{4,14},{6,12},{8,2},{10,0},{12,6},{14,4},{1,11},{3,9}... | collective-permute-start | bytes 540680 | tf_op jit(solution)/shard_map/ppermute | solution.py:356
  21.8 16.4 %collective-permute-start.36 = (bf16[88,1024]{1,0:T(8,128)(2,1)S(1)}, bf16[88,1024]{1,0:T(8,128)(2,1)S(1)}, u32[]{:S(2)}, u32[]{:S(2)}) collective-permute-start(bf16[88,1024]{1,0:T(8,128)(2,1)S(1)} %get-tuple-element.185), channel_id=1, source_target_pairs={{0,14},{2,12},{4,10},{6,8},{8,6},{10,4},{12,2},{14,0},{1,15},{3,13... | collective-permute-start | bytes 540680 | tf_op jit(solution)/shard_map/ppermute | solution.py:356
  38.3 3.3 %collective-permute-start.37 = (bf16[704,1024]{1,0:T(8,128)(2,1)S(1)}, bf16[704,1024]{1,0:T(8,128)(2,1)S(1)}, u32[]{:S(2)}, u32[]{:S(2)}) collective-permute-start(bf16[704,1024]{1,0:T(8,128)(2,1)S(1)} %join.7.own_ref), channel_id=1, source_target_pairs={{0,1},{1,0},{2,3},{3,2},{4,5},{5,4},{6,7},{7,6},{8,9},{9,8},{10,11... | collective-permute-start | bytes 4325384 | tf_op jit(solution)/shard_map/ppermute | solution.py:371
  40.5 2.9 %copy-start = (s32[4096]{0:T(1024)S(1)}, s32[4096]{0:T(1024)}, u32[]{:S(2)}) copy-start(s32[4096]{0:T(1024)} %param.13) | copy-start | bytes 49156
  40.5 2.9 %copy-start.1 = (f32[512,1024]{1,0:T(8,128)S(1)}, f32[512,1024]{1,0:T(8,128)}, u32[]{:S(2)}) copy-start(f32[512,1024]{1,0:T(8,128)} %emb_hbm.1) | copy-start | bytes 6291460
  40.5 2.9 %copy-start.2 = (s32[512]{0:T(512)S(1)}, s32[512]{0:T(512)}, u32[]{:S(2)}) copy-start(s32[512]{0:T(512)} %param.11) | copy-start | bytes 6148
  40.5 2.9 %copy-start.3 = (s32[512]{0:T(512)S(1)}, s32[512]{0:T(512)}, u32[]{:S(2)}) copy-start(s32[512]{0:T(512)} %param.12) | copy-start | bytes 6148
